TPU v7x, 128 devices: a whole 4x4x4 slice. The times are simulated.
128 devices in a mesh: row: 2 (over core), seq: 64 (over z, y, x).
Axes of the slice: x: 4, y: 4, z: 4, core: 2. Of those that a mesh axis runs over, the one named last changes fastest.
Arguments:
- tokens: bfloat16 [4, 4096, 2048], P('row', 'seq'), may hold values from -6 to 6
- lengths: int32 [4, 4], P('row'), may hold values from 0 to 4096, as said below
- norm_one: bfloat16 [2048], P(('row', 'seq')), may hold values from 0.5 to 1.5
- gelu_weight: bfloat16 [2048, 2816], P(('row', 'seq')), may hold values from -0.125 to 0.125
- input_weight: bfloat16 [2048, 2816], P(('row', 'seq')), may hold values from -0.125 to 0.125
- conv_weight: bfloat16 [2816, 4], P(('row', 'seq')), may hold values from -3 to 3
- conv_bias: bfloat16 [2816], P(('row', 'seq')), may hold values from -3 to 3
- gate_input: bfloat16 [2816, 176], P(('row', 'seq')), may hold values from -0.4375 to 0.4375
- bias_input: bfloat16 [2816], P(('row', 'seq')), may hold values from -4 to 4
- gate_recur: bfloat16 [2816, 176], P(('row', 'seq')), may hold values from -0.4375 to 0.4375
- bias_recur: bfloat16 [2816], P(('row', 'seq')), may hold values from -4 to 4
- decay_param: bfloat16 [2816], P(('row', 'seq')), may hold values from -12 to -3
- out_weight: bfloat16 [2816, 2048], P(('row', 'seq')), may hold values from -0.109375 to 0.109375
- norm_two: bfloat16 [2048], P(('row', 'seq')), may hold values from 0.5 to 1.5
- gate_weight: bfloat16 [2048, 6144], P(('row', 'seq')), may hold values from -0.125 to 0.125
- up_weight: bfloat16 [2048, 6144], P(('row', 'seq')), may hold values from -0.125 to 0.125
- down_weight: bfloat16 [6144, 2048], P(('row', 'seq')), may hold values from -0.078125 to 0.078125
- cotangent: bfloat16 [4, 4096, 2048], P('row', 'seq'), may hold values from -6 to 6
Outputs:
- output: bfloat16 [4, 4096, 2048], P('row', 'seq')
- grad_tokens: float32 [4, 4096, 2048], P('row', 'seq')
- grad_norm_one: float32 [2048], P(('row', 'seq'))
- grad_gelu_weight: float32 [2048, 2816], P(('row', 'seq'))
- grad_input_weight: float32 [2048, 2816], P(('row', 'seq'))
- grad_conv_weight: float32 [2816, 4], P(('row', 'seq'))
- grad_conv_bias: float32 [2816], P(('row', 'seq'))
- grad_gate_input: float32 [2816, 176], P(('row', 'seq'))
- grad_bias_input: float32 [2816], P(('row', 'seq'))
- grad_gate_recur: float32 [2816, 176], P(('row', 'seq'))
- grad_bias_recur: float32 [2816], P(('row', 'seq'))
- grad_decay_param: float32 [2816], P(('row', 'seq'))
- grad_out_weight: float32 [2816, 2048], P(('row', 'seq'))
- grad_norm_two: float32 [2048], P(('row', 'seq'))
- grad_gate_weight: float32 [2048, 6144], P(('row', 'seq'))
- grad_up_weight: float32 [2048, 6144], P(('row', 'seq'))
- grad_down_weight: float32 [6144, 2048], P(('row', 'seq'))
Inputs may be any that keep to these rules, and one draw needn't show every extreme that they name: Each row lists its sequences' lengths in order, each of 1024 tokens or more, then zeros; they sum to at most 4096, the remaining slots of the row being padding. Among the 2 rows of each index of row, one holds a single sequence of 4096 tokens.
All inputs are finite; a program needn't handle non-finite values.
Results may differ from a plain program's by a relative error of at most 0.012.
The roundings to bfloat16 on the way count: a program that leaves them out, or rounds other values in their place, can miss the bound.
Values may be sent and summed in bfloat16 or wider, within the bound.
No kernel may reach another device: no remote copies, remote signals or barrier semaphores. Data moves between devices by JAX's collectives and lax.ppermute only.
A program may use at most 512 MiB of HBM per device.

v0:
```python
from functools import partial

import jax
import jax.numpy as jnp
from jax import lax
from jax.sharding import PartitionSpec as P

epsilon = 1e-06
beta_floor = 0.001
rim_width = 3


def shifted(block, axis, distance):
    devices = range(lax.axis_size(axis))
    route = [(i - distance, i) for i in devices if i - distance in devices]
    return lax.ppermute(block, axis, route)


def carried_in(value, axis, join, neutral, backward):
    count, mine = (lax.axis_size(axis), lax.axis_index(axis))
    pieces = jax.tree.map(lambda part: lax.all_gather(part, axis), value)
    if backward:
        pieces = jax.tree.map(lambda part: part[::-1], pieces)
        mine = count - 1 - mine
    subtotal = jax.tree.map(
        lambda part, zero: jnp.full_like(part, 0) + jnp.asarray(zero, part.dtype), value, neutral
    )

    def step(position, subtotal):
        longer = join(subtotal, jax.tree.map(lambda part: part[position], pieces))
        return jax.tree.map(lambda new, old: jnp.where(position < mine, new, old), longer, subtotal)

    return lax.fori_loop(0, count - 1, step, subtotal)


def chain_combine(earlier, later):
    return (earlier[0] * later[0], later[0] * earlier[1] + later[1])


def rms_scale(values, gain):
    return values * lax.rsqrt(jnp.mean(values * values, axis=-1, keepdims=True) + epsilon) * gain


def gated_inputs(reset_flag, raw_input, raw_recur, values, bias_input, bias_recur, decay_param):
    gate_in = jax.nn.sigmoid(raw_input + bias_input)
    gate_rec = jax.nn.sigmoid(raw_recur + bias_recur)
    log_decay = -8.0 * gate_rec * jax.nn.softplus(decay_param)
    factor = jnp.exp(log_decay) * (1.0 - reset_flag)
    root = jnp.sqrt(jnp.maximum(-jnp.expm1(2.0 * log_decay), beta_floor))
    return (factor, root * gate_in * values)


def gelu_product(left, right):
    return jax.nn.gelu(left) * right


def project_in(left, weight):
    return jnp.dot(left, weight, preferred_element_type=jnp.float32)


def project_back(grad, weight):
    return lax.dot_general(
        grad, weight, (((1,), (1,)), ((), ())), preferred_element_type=jnp.float32
    )


def outer_sum(left, grad):
    return lax.dot_general(left, grad, (((0,), (0,)), ((), ())), preferred_element_type=jnp.float32)


def segment_tables(lengths, first_slot, stretch_len):
    slot_index = first_slot - rim_width + jnp.arange(stretch_len + 2 * rim_width, dtype=jnp.int32)
    seg_starts = jnp.cumsum(lengths, axis=1) - lengths
    seg_live = lengths > 0
    before = seg_live[:, None, :] & (seg_starts[:, None, :] <= slot_index[None, :, None])
    begins = seg_live[:, None, :] & (seg_starts[:, None, :] == slot_index[None, :, None])
    segment = jnp.sum(before.astype(jnp.int32), axis=2)
    reset_flag = jnp.sum(begins.astype(jnp.int32), axis=2).astype(jnp.float32)
    row_total = jnp.sum(lengths, axis=1)
    valid_mask = (slot_index[None, :] < row_total[:, None]).astype(jnp.float32)
    return (segment, reset_flag, valid_mask)


def body(
    tokens,
    lengths,
    norm_one,
    gelu_weight,
    input_weight,
    conv_weight,
    conv_bias,
    gate_input,
    bias_input,
    gate_recur,
    bias_recur,
    decay_param,
    out_weight,
    norm_two,
    gate_weight,
    up_weight,
    down_weight,
    cotangent,
):
    row_count, stretch_len, model_width = tokens.shape
    token_count = row_count * stretch_len
    seq_place = lax.axis_index("seq")
    first_slot = seq_place * stretch_len
    segment, reset_all, valid_all = segment_tables(lengths, first_slot, stretch_len)
    reset_flag = reset_all[:, rim_width : rim_width + stretch_len][:, :, None]
    valid_mask = valid_all[:, rim_width : rim_width + stretch_len].reshape(token_count, 1)
    current_seg = segment[:, rim_width : rim_width + stretch_len]
    shards = (
        norm_one,
        gelu_weight,
        input_weight,
        conv_weight,
        conv_bias,
        gate_input,
        bias_input,
        gate_recur,
        bias_recur,
        decay_param,
        out_weight,
        norm_two,
    )
    gathered = (
        lax.all_gather(shards[0], ("row", "seq"), axis=0, tiled=True),
        lax.all_gather(shards[1], ("row", "seq"), axis=0, tiled=True),
        lax.all_gather(shards[2], ("row", "seq"), axis=0, tiled=True),
        lax.all_gather(shards[3], ("row", "seq"), axis=0, tiled=True),
        lax.all_gather(shards[4], ("row", "seq"), axis=0, tiled=True),
        lax.all_gather(shards[5], ("row", "seq"), axis=0, tiled=True),
        lax.all_gather(shards[6], ("row", "seq"), axis=0, tiled=True),
        lax.all_gather(shards[7], ("row", "seq"), axis=0, tiled=True),
        lax.all_gather(shards[8], ("row", "seq"), axis=0, tiled=True),
        lax.all_gather(shards[9], ("row", "seq"), axis=0, tiled=True),
        lax.all_gather(shards[10], ("row", "seq"), axis=0, tiled=True),
        lax.all_gather(shards[11], ("row", "seq"), axis=0, tiled=True),
    )
    gain_one = gathered[0].astype(jnp.float32)
    conv_taps = gathered[3].astype(jnp.float32)
    conv_shift = gathered[4].astype(jnp.float32)
    gain_two = gathered[11].astype(jnp.float32)
    hidden_width, head_size = gathered[5].shape
    head_count = hidden_width // head_size
    tap_count = conv_taps.shape[1]
    flat_tokens = tokens.reshape(token_count, model_width).astype(jnp.float32)
    normed_full, pull_norm_one = jax.vjp(rms_scale, flat_tokens, gain_one)
    normed = normed_full.astype(jnp.bfloat16)
    gelu_pre = project_in(normed, gathered[1])
    conv_in = (
        project_in(normed, gathered[2])
        .astype(jnp.bfloat16)
        .reshape(row_count, stretch_len, hidden_width)
    )
    rim_before = shifted(conv_in[:, stretch_len - rim_width :, :], "seq", 1)
    extended = jnp.concatenate([rim_before, conv_in], axis=1).astype(jnp.float32)
    conv_out = conv_shift + conv_taps[:, 0] * extended[:, rim_width:]
    same_list = [jnp.ones((row_count, stretch_len, 1), jnp.float32)]
    for offset in range(1, tap_count):
        same_seg = segment[:, rim_width - offset : rim_width - offset + stretch_len] == current_seg
        same_seg = same_seg.astype(jnp.float32)[:, :, None]
        same_list.append(same_seg)
        conv_out = (
            conv_out
            + conv_taps[:, offset]
            * extended[:, rim_width - offset : rim_width - offset + stretch_len]
            * same_seg
        )
    conv_vals = conv_out.astype(jnp.bfloat16)
    conv_float = conv_vals.astype(jnp.float32)
    blocks = conv_vals.reshape(token_count, head_count, head_size)
    input_blocks = gathered[5].reshape(head_count, head_size, head_size)
    recur_blocks = gathered[7].reshape(head_count, head_size, head_size)
    raw_input = jnp.einsum("thk,hkj->thj", blocks, input_blocks, preferred_element_type=jnp.float32)
    raw_recur = jnp.einsum("thk,hkj->thj", blocks, recur_blocks, preferred_element_type=jnp.float32)
    raw_input = raw_input.reshape(row_count, stretch_len, hidden_width)
    raw_recur = raw_recur.reshape(row_count, stretch_len, hidden_width)
    (factor, drive_in), pull_gates = jax.vjp(
        partial(gated_inputs, reset_flag),
        raw_input,
        raw_recur,
        conv_float,
        gathered[6].astype(jnp.float32),
        gathered[8].astype(jnp.float32),
        gathered[9].astype(jnp.float32),
    )
    cumulative, local_state = lax.associative_scan(chain_combine, (factor, drive_in), axis=1)
    ones_carry = jnp.ones((row_count, hidden_width), jnp.float32)
    zeros_carry = jnp.zeros((row_count, hidden_width), jnp.float32)
    carried = carried_in(
        (cumulative[:, -1], local_state[:, -1]),
        "seq",
        chain_combine,
        (ones_carry, zeros_carry),
        False,
    )
    entering = carried[1]
    rec_state = local_state + cumulative * entering[:, None, :]
    state_flat = rec_state.reshape(token_count, hidden_width)
    mixed_full, pull_mix = jax.vjp(gelu_product, gelu_pre, state_flat)
    mixed = mixed_full.astype(jnp.bfloat16)
    middle = flat_tokens + project_in(mixed, gathered[10])
    normed_two_full, pull_norm_two = jax.vjp(rms_scale, middle, gain_two)
    normed_two = normed_two_full.astype(jnp.bfloat16)
    upstream = cotangent.reshape(token_count, model_width).astype(jnp.float32) * valid_mask
    grad_down = upstream.astype(jnp.bfloat16)
    mlp_full = (
        lax.all_gather(gate_weight, ("row", "seq"), axis=0, tiled=True),
        lax.all_gather(up_weight, ("row", "seq"), axis=0, tiled=True),
        lax.all_gather(down_weight, ("row", "seq"), axis=0, tiled=True),
    )
    gate_pre = project_in(normed_two, mlp_full[0])
    up_pre = project_in(normed_two, mlp_full[1])
    inner_full, pull_inner = jax.vjp(gelu_product, gate_pre, up_pre)
    inner_act = inner_full.astype(jnp.bfloat16)
    down_out = project_in(inner_act, mlp_full[2])
    result = (middle + down_out) * valid_mask
    output = result.reshape(row_count, stretch_len, model_width).astype(jnp.bfloat16)
    mlp_params = (
        lax.all_gather(gate_weight, ("row", "seq"), axis=0, tiled=True),
        lax.all_gather(up_weight, ("row", "seq"), axis=0, tiled=True),
        lax.all_gather(down_weight, ("row", "seq"), axis=0, tiled=True),
    )
    grad_down_weight = outer_sum(inner_act, grad_down)
    grad_inner = project_back(grad_down, mlp_params[2])
    grad_gate_pre, grad_up_pre = pull_inner(grad_inner)
    grad_gate = grad_gate_pre.astype(jnp.bfloat16)
    grad_up = grad_up_pre.astype(jnp.bfloat16)
    grad_gate_weight = outer_sum(normed_two, grad_gate)
    grad_up_weight = outer_sum(normed_two, grad_up)
    grad_normed_two = project_back(grad_gate, mlp_params[0]) + project_back(grad_up, mlp_params[1])
    mlp_sums = (
        lax.psum_scatter(grad_gate_weight, ("row", "seq"), scatter_dimension=0, tiled=True),
        lax.psum_scatter(grad_up_weight, ("row", "seq"), scatter_dimension=0, tiled=True),
        lax.psum_scatter(grad_down_weight, ("row", "seq"), scatter_dimension=0, tiled=True),
    )
    grad_middle_norm, grad_norm_two = pull_norm_two(grad_normed_two)
    grad_middle = upstream + grad_middle_norm
    grad_branch = grad_middle.astype(jnp.bfloat16)
    recur_params = (
        lax.all_gather(gelu_weight, ("row", "seq"), axis=0, tiled=True),
        lax.all_gather(input_weight, ("row", "seq"), axis=0, tiled=True),
        lax.all_gather(conv_weight, ("row", "seq"), axis=0, tiled=True),
        lax.all_gather(gate_input, ("row", "seq"), axis=0, tiled=True),
        lax.all_gather(gate_recur, ("row", "seq"), axis=0, tiled=True),
        lax.all_gather(out_weight, ("row", "seq"), axis=0, tiled=True),
    )
    back_taps = recur_params[2].astype(jnp.float32)
    back_input_blocks = recur_params[3].reshape(head_count, head_size, head_size)
    back_recur_blocks = recur_params[4].reshape(head_count, head_size, head_size)
    grad_out_weight = outer_sum(mixed, grad_branch)
    grad_mixed = project_back(grad_branch, recur_params[5])
    grad_gelu_pre, grad_state = pull_mix(grad_mixed)
    grad_gelu = grad_gelu_pre.astype(jnp.bfloat16)
    grad_state = grad_state.reshape(row_count, stretch_len, hidden_width)
    next_factor = jnp.concatenate([factor[:, 1:], jnp.ones_like(factor[:, :1])], axis=1)
    reach_prod, adjoint_local = lax.associative_scan(
        chain_combine, (next_factor, grad_state), reverse=True, axis=1
    )
    message = (factor[:, 0] * reach_prod[:, 0], factor[:, 0] * adjoint_local[:, 0])
    arriving = carried_in(message, "seq", chain_combine, (ones_carry, zeros_carry), True)
    adjoint = adjoint_local + reach_prod * arriving[1][:, None, :]
    previous = jnp.concatenate([entering[:, None, :], rec_state[:, :-1]], axis=1)
    (
        grad_raw_input,
        grad_raw_recur,
        grad_conv_direct,
        grad_bias_input,
        grad_bias_recur,
        grad_decay_param,
    ) = pull_gates((adjoint * previous, adjoint))
    grad_in16 = grad_raw_input.reshape(token_count, head_count, head_size).astype(jnp.bfloat16)
    grad_rec16 = grad_raw_recur.reshape(token_count, head_count, head_size).astype(jnp.bfloat16)
    grad_gate_input = jnp.einsum(
        "thk,thj->hkj", blocks, grad_in16, preferred_element_type=jnp.float32
    ).reshape(hidden_width, head_size)
    grad_gate_recur = jnp.einsum(
        "thk,thj->hkj", blocks, grad_rec16, preferred_element_type=jnp.float32
    ).reshape(hidden_width, head_size)
    grad_conv_gates = jnp.einsum(
        "thj,hkj->thk", grad_in16, back_input_blocks, preferred_element_type=jnp.float32
    )
    grad_conv_gates = grad_conv_gates + jnp.einsum(
        "thj,hkj->thk", grad_rec16, back_recur_blocks, preferred_element_type=jnp.float32
    )
    grad_conv = (
        grad_conv_direct + grad_conv_gates.reshape(row_count, stretch_len, hidden_width)
    ).astype(jnp.bfloat16)
    rim_ahead = shifted(grad_conv[:, :rim_width], "seq", -1)
    grad_extended = jnp.concatenate([grad_conv, rim_ahead], axis=1).astype(jnp.float32)
    grad_conv_float = grad_conv.astype(jnp.float32)
    grad_conv_bias = jnp.sum(grad_conv_float, axis=(0, 1))
    tap_grads = [jnp.sum(grad_conv_float * extended[:, rim_width:], axis=(0, 1))]
    grad_conv_in = back_taps[:, 0] * grad_conv_float
    for offset in range(1, tap_count):
        tap_grads.append(
            jnp.sum(
                grad_conv_float
                * extended[:, rim_width - offset : rim_width - offset + stretch_len]
                * same_list[offset],
                axis=(0, 1),
            )
        )
        ahead_seg = segment[:, rim_width + offset : rim_width + offset + stretch_len] == current_seg
        ahead_seg = ahead_seg.astype(jnp.float32)[:, :, None]
        grad_conv_in = (
            grad_conv_in
            + back_taps[:, offset] * grad_extended[:, offset : offset + stretch_len] * ahead_seg
        )
    grad_conv_weight = jnp.stack(tap_grads, axis=1)
    grad_input16 = grad_conv_in.reshape(token_count, hidden_width).astype(jnp.bfloat16)
    grad_gelu_weight = outer_sum(normed, grad_gelu)
    grad_input_weight = outer_sum(normed, grad_input16)
    grad_normed = project_back(grad_gelu, recur_params[0]) + project_back(
        grad_input16, recur_params[1]
    )
    grad_flat_norm, grad_norm_one = pull_norm_one(grad_normed)
    grad_tokens = (grad_middle + grad_flat_norm).reshape(row_count, stretch_len, model_width)
    recur_sums = (
        lax.psum_scatter(grad_norm_one, ("row", "seq"), scatter_dimension=0, tiled=True),
        lax.psum_scatter(grad_gelu_weight, ("row", "seq"), scatter_dimension=0, tiled=True),
        lax.psum_scatter(grad_input_weight, ("row", "seq"), scatter_dimension=0, tiled=True),
        lax.psum_scatter(grad_conv_weight, ("row", "seq"), scatter_dimension=0, tiled=True),
        lax.psum_scatter(grad_conv_bias, ("row", "seq"), scatter_dimension=0, tiled=True),
        lax.psum_scatter(grad_gate_input, ("row", "seq"), scatter_dimension=0, tiled=True),
        lax.psum_scatter(grad_bias_input, ("row", "seq"), scatter_dimension=0, tiled=True),
        lax.psum_scatter(grad_gate_recur, ("row", "seq"), scatter_dimension=0, tiled=True),
        lax.psum_scatter(grad_bias_recur, ("row", "seq"), scatter_dimension=0, tiled=True),
        lax.psum_scatter(grad_decay_param, ("row", "seq"), scatter_dimension=0, tiled=True),
        lax.psum_scatter(grad_out_weight, ("row", "seq"), scatter_dimension=0, tiled=True),
        lax.psum_scatter(grad_norm_two, ("row", "seq"), scatter_dimension=0, tiled=True),
    )
    return (
        output,
        grad_tokens,
        recur_sums[0],
        recur_sums[1],
        recur_sums[2],
        recur_sums[3],
        recur_sums[4],
        recur_sums[5],
        recur_sums[6],
        recur_sums[7],
        recur_sums[8],
        recur_sums[9],
        recur_sums[10],
        recur_sums[11],
        mlp_sums[0],
        mlp_sums[1],
        mlp_sums[2],
    )


def solution(mesh):
    return jax.shard_map(
        body,
        mesh=mesh,
        in_specs=(
            P("row", "seq", None),
            P("row", None),
            P(("row", "seq")),
            P(("row", "seq"), None),
            P(("row", "seq"), None),
            P(("row", "seq"), None),
            P(("row", "seq")),
            P(("row", "seq"), None),
            P(("row", "seq")),
            P(("row", "seq"), None),
            P(("row", "seq")),
            P(("row", "seq")),
            P(("row", "seq"), None),
            P(("row", "seq")),
            P(("row", "seq"), None),
            P(("row", "seq"), None),
            P(("row", "seq"), None),
            P("row", "seq", None),
        ),
        out_specs=(
            P("row", "seq", None),
            P("row", "seq", None),
            P(("row", "seq")),
            P(("row", "seq"), None),
            P(("row", "seq"), None),
            P(("row", "seq"), None),
            P(("row", "seq")),
            P(("row", "seq"), None),
            P(("row", "seq")),
            P(("row", "seq"), None),
            P(("row", "seq")),
            P(("row", "seq")),
            P(("row", "seq"), None),
            P(("row", "seq")),
            P(("row", "seq"), None),
            P(("row", "seq"), None),
            P(("row", "seq"), None),
        ),
        check_vma=False,
    )
```

profile of v0, /device:TPU:1, one launch (start us, length us, event | category | flops | bytes accessed | tf_op | source)
XLA Modules:
  0.0 4728.6 jit_solution(17752027896479327238)
XLA Ops:
  13.9 69.9 %all-reduce.70 = (bf16[2816]{0:T(1024)(128)(2,1)S(1)}, bf16[2048]{0:T(1024)(128)(2,1)S(1)}, bf16[2816]{0:T(1024)(128)(2,1)S(1)}, bf16[2816]{0:T(1024)(128)(2,1)S...) all-reduce(bf16[2816]{0:T(1024)(128)(2,1)S(1)} %dynamic-update-slic, ...), channel_id=1, replica_groups=mesh['row'=2,'seq'=64] {'row','seq'}, use_global_device_ids=true, to_apply=%add.53 | all-reduce | flops 15360 | bytes 61440
  85.7 314.9 %all-gather.4 = bf16[128,22,4]{1,2,0:T(4,128)(2,1)S(1)} all-gather(bf16[1,22,4]{1,2,0:T(4,128)(2,1)} %bitcast.171), channel_id=1, replica_groups=mesh['row'=2,'seq'=64] {'row','seq'}, dimensions={0}, use_global_device_ids=true | all-gather | bytes 22704 | tf_op jit(solution)/shard_map/all_gather | solution.py:130
  404.2 338.3 %all-gather.5 = bf16[128,22,176]{2,1,0:T(8,128)(2,1)} all-gather(bf16[1,22,176]{2,1,0:T(8,128)(2,1)S(1)} %bitcast.169), channel_id=1, replica_groups=mesh['row'=2,'seq'=64] {'row','seq'}, dimensions={0}, use_global_device_ids=true | all-gather | bytes 998976 | tf_op jit(solution)/shard_map/all_gather | solution.py:134
  742.5 321.2 %all-gather.6 = bf16[128,22,176]{2,1,0:T(8,128)(2,1)S(1)} all-gather(bf16[1,22,176]{2,1,0:T(8,128)(2,1)S(1)} %bitcast.170), channel_id=1, replica_groups=mesh['row'=2,'seq'=64] {'row','seq'}, dimensions={0}, use_global_device_ids=true | all-gather | bytes 998976 | tf_op jit(solution)/shard_map/all_gather | solution.py:132
  1253.5 15.2 reshape.259
  1281.6 11.0 slice.531
  1292.6 11.0 slice.538
  1303.5 11.1 slice.529
  1323.6 34.7 all-gather.29.cloned.1.call-done
  1367.2 51.1 %while.28 = (s32[]{:T(128)}, f32[2,2816]{1,0:T(2,128)S(1)}, s32[]{:T(128)}, f32[64,2,2816]{2,1,0:T(2,128)}, f32[64,2,2816]{2,1,0:T(2,128)}, /*index=5*/s32[]{:T(128)}, s32[]{:T(128)}) while((s32[]{:T(128)}, f32[2,2816]{1,0:T(2,128)S(1)}, s32[]{:T(128)}, f32[64,2,2816]{2,1,0:T(2,128)}, f32[64,2,2816]{2,1,0:T(2,128)}, ...), condition=%wide.region_5.6_spmd.clone, body=%wide.region_4.5_spmd.clone.sunk | while | flops 22532 | bytes 90213 | solution.py:33
  1422.8 10.2 all-gather.19.cloned.1.call-done
  1433.0 8.0 fusion.41
  1449.4 78.9 %all-gather.23.cloned.1.call-done = bf16[2048,6144]{1,0:T(8,128)(2,1)} async-done(((bf16[16,6144]{1,0:T(8,128)(2,1)}), bf16[2048,6144]{1,0:T(8,128)(2,1)}) %all-gather.23.cloned.1.call-update) | async-done | bytes 25165840 | tf_op jit(solution)/shard_map/all_gather | solution.py:209
  1528.2 13.5 fusion.103
  1541.7 82.1 %all-gather.25.cloned.1.call-done = bf16[2048,6144]{1,0:T(8,128)(2,1)} async-done(((bf16[16,6144]{1,0:T(8,128)(2,1)}), bf16[2048,6144]{1,0:T(8,128)(2,1)}) %all-gather.25.cloned.1.call-update) | async-done | bytes 25165840 | tf_op jit(solution)/shard_map/all_gather | solution.py:210
  1623.8 13.4 fusion.104
  1637.3 82.2 %all-gather.27.cloned.1.call-done = bf16[6144,2048]{1,0:T(8,128)(2,1)} async-done(((bf16[48,2048]{1,0:T(8,128)(2,1)}), bf16[6144,2048]{1,0:T(8,128)(2,1)}) %all-gather.27.cloned.1.call-update) | async-done | bytes 25165840 | tf_op jit(solution)/shard_map/all_gather | solution.py:211
  1719.4 17.8 multiply_convert_fusion
  1737.2 14.4 fusion.105
  1751.6 16.1 multiply_reduce_fusion.1
  1770.3 10.2 fusion.56
  1787.3 11.0 slice.533
  1798.3 11.0 slice.535
  1918.7 11.0 slice.575
  1949.8 12.0 rev.15
  1961.8 11.9 rev.14
  1973.7 9.3 fusion.106
  1983.0 23.7 all-gather.33.cloned.1.call-done
  2018.2 53.7 %all-gather.35.cloned.1.call-done = f32[128,1,2816]{2,1,0:T(1,128)} async-done(((f32[2,1,2816]{2,1,0:T(1,128)}), f32[128,1,2816]{2,1,0:T(1,128)}) %all-gather.35.cloned.1.call-update) | async-done | bytes 1441808 | tf_op jit(solution)/shard_map/all_gather | solution.py:21
  2083.6 50.9 %while.29 = (s32[]{:T(128)}, f32[2,2816]{1,0:T(2,128)S(1)}, s32[]{:T(128)}, f32[64,2,2816]{2,1,0:T(2,128)}, f32[64,2,2816]{2,1,0:T(2,128)}, /*index=5*/s32[]{:T(128)}, s32[]{:T(128)}) while((s32[]{:T(128)}, f32[2,2816]{1,0:T(2,128)S(1)}, s32[]{:T(128)}, f32[64,2,2816]{2,1,0:T(2,128)}, f32[64,2,2816]{2,1,0:T(2,128)}, ...), condition=%wide.region_10.11_spmd.clone, body=%wide.region_9.10_spmd.clone.sunk | while | flops 22532 | bytes 90213 | solution.py:33
  2134.7 6.6 multiply_reduce_fusion
  2185.4 9.3 fusion.107
  2195.4 9.5 convolution_bitcast_fusion
  2206.0 20.9 fusion.110
  2227.1 20.8 fusion.111
  2249.4 19.5 fusion.112
  2270.3 9.5 fusion.64
  2284.1 491.8 %fusion.89 = (f32[24,176]{1,0:T(8,128)S(1)}, f32[24,176]{1,0:T(8,128)S(1)}, f32[24,2048]{1,0:T(8,128)S(1)}) fusion(f32[2816,176]{1,0:T(8,128)} %bitcast.137, f32[2816,176]{1,0:T(8,128)} %bitcast.138, f32[2816,2048]{1,0:T(8,128)} %fusion.64), kind=kCustom, calls=%all-reduce-scatter.3 | all-reduce-scatter fusion | flops 7372801 | bytes 27264000
  2779.8 12.8 collective-permute-start.12
  2804.4 11.6 collective-permute-start.16
  2845.2 13.0 fusion.13
  2916.7 8.0 collective-permute-done.31
  2924.7 19.2 concatenate.98
  2945.6 141.8 %reduce-scatter.13.cloned.1.call-done = f32[16,2816]{1,0:T(8,128)} async-done(((f32[2048,2816]{1,0:T(8,128)}), f32[16,2816]{1,0:T(8,128)}) %reduce-scatter.13.cloned.1.call-update) | async-done | bytes 180240 | tf_op jit(solution)/shard_map/reduce_scatter | solution.py:322
  3087.4 695.8 %reduce-scatter.15.cloned.1.call-done = f32[16,2816]{1,0:T(8,128)} async-done(((f32[2048,2816]{1,0:T(8,128)}), f32[16,2816]{1,0:T(8,128)}) %reduce-scatter.15.cloned.1.call-update) | async-done | bytes 180240 | tf_op jit(solution)/shard_map/reduce_scatter | solution.py:323
  3783.2 310.0 %reduce-scatter.17.cloned.1.call-done = f32[16,6144]{1,0:T(8,128)} async-done(((f32[2048,6144]{1,0:T(8,128)}), f32[16,6144]{1,0:T(8,128)}) %reduce-scatter.17.cloned.1.call-update) | async-done | bytes 393232 | tf_op jit(solution)/shard_map/reduce_scatter | solution.py:234
  4093.2 314.3 %reduce-scatter.19.cloned.1.call-done = f32[16,6144]{1,0:T(8,128)} async-done(((f32[2048,6144]{1,0:T(8,128)}), f32[16,6144]{1,0:T(8,128)}) %reduce-scatter.19.cloned.1.call-update) | async-done | bytes 393232 | tf_op jit(solution)/shard_map/reduce_scatter | solution.py:235
  4407.5 314.3 %reduce-scatter.21.cloned.1.call-done = f32[48,2048]{1,0:T(8,128)} async-done(((f32[6144,2048]{1,0:T(8,128)}), f32[48,2048]{1,0:T(8,128)}) %reduce-scatter.21.cloned.1.call-update) | async-done | bytes 393232 | tf_op jit(solution)/shard_map/reduce_scatter | solution.py:236
  (750 shorter events, 663.6 us)
Async XLA Ops:
  7.2 1056.5 %all-gather.21.cloned.1.call-start = ((), (), s32[]{:S(2)}) async-start(), calls=%async_computation.6 | async-start | bytes 11624448 | tf_op jit(solution)/shard_map/all_gather | solution.py:129
  8.0 1245.5 %all-gather.37.cloned.1.call-start = ((), (), s32[]{:S(2)}) async-start(), calls=%async_computation.19 | async-start | bytes 12681216 | tf_op jit(solution)/shard_map/all_gather | solution.py:137
  8.7 1305.9 %all-gather.31.cloned.1.call-start = ((), (), s32[]{:S(2)}) async-start(), calls=%async_computation.16 | async-start | bytes 1464320 | tf_op jit(solution)/shard_map/all_gather | solution.py:21
  1234.9 123.4 %all-gather.29.cloned.1.call-start = ((), (), s32[]{:S(2)}) async-start(), calls=%async_computation.15 | async-start | bytes 1464320 | tf_op jit(solution)/shard_map/all_gather | solution.py:21
  1248.5 184.4 %all-gather.19.cloned.1.call-start = ((), (), s32[]{:S(2)}) async-start(), calls=%async_computation.5 | async-start | bytes 11624448 | tf_op jit(solution)/shard_map/all_gather | solution.py:128
  1249.1 279.1 %all-gather.23.cloned.1.call-start = ((), (), s32[]{:S(2)}) async-start(), calls=%async_computation.7 | async-start | bytes 25362432 | tf_op jit(solution)/shard_map/all_gather | solution.py:209
  1249.7 374.1 %all-gather.25.cloned.1.call-start = ((), (), s32[]{:S(2)}) async-start(), calls=%async_computation.8 | async-start | bytes 25362432 | tf_op jit(solution)/shard_map/all_gather | solution.py:210
  1250.5 469.0 %all-gather.27.cloned.1.call-start = ((), (), s32[]{:S(2)}) async-start(), calls=%async_computation.9 | async-start | bytes 25362432 | tf_op jit(solution)/shard_map/all_gather | solution.py:211
  1251.2 755.5 %all-gather.33.cloned.1.call-start = ((), (), s32[]{:S(2)}) async-start(), calls=%async_computation.17 | async-start | bytes 1464320 | tf_op jit(solution)/shard_map/all_gather | solution.py:21
  1944.6 127.3 %all-gather.35.cloned.1.call-start = ((), (), s32[]{:S(2)}) async-start(), calls=%async_computation.18 | async-start | bytes 1464320 | tf_op jit(solution)/shard_map/all_gather | solution.py:21
  1945.2 962.6 %all-reduce.74.cloned.1.call-start = ((), (), s32[]{:S(2)}) async-start(), calls=%async_computation.20 | async-start | bytes 221184
  2185.4 902.1 %reduce-scatter.13.cloned.1.call-start = ((), (), s32[]{:S(2)}) async-start(), calls=%async_computation.10 | async-start | bytes 23248896 | tf_op jit(solution)/shard_map/reduce_scatter | solution.py:322
  2194.8 1588.4 %reduce-scatter.15.cloned.1.call-start = ((), (), s32[]{:S(2)}) async-start(), calls=%async_computation.11 | async-start | bytes 23248896 | tf_op jit(solution)/shard_map/reduce_scatter | solution.py:323
  2205.0 1888.3 %reduce-scatter.17.cloned.1.call-start = ((), (), s32[]{:S(2)}) async-start(), calls=%async_computation.12 | async-start | bytes 50724864 | tf_op jit(solution)/shard_map/reduce_scatter | solution.py:234
  2226.9 2180.7 %reduce-scatter.19.cloned.1.call-start = ((), (), s32[]{:S(2)}) async-start(), calls=%async_computation.13 | async-start | bytes 50724864 | tf_op jit(solution)/shard_map/reduce_scatter | solution.py:235
  2247.9 2473.9 %reduce-scatter.21.cloned.1.call-start = ((), (), s32[]{:S(2)}) async-start(), calls=%async_computation.14 | async-start | bytes 50724864 | tf_op jit(solution)/shard_map/reduce_scatter | solution.py:236
  2775.9 42.0 collective-permute-start.13
  2777.9 26.5 collective-permute-start.23
  2779.8 36.2 collective-permute-start.12
  2792.6 29.3 collective-permute-start.14
  2798.2 26.0 collective-permute-start.15
  2804.4 22.0 collective-permute-start.16
  2816.0 12.4 collective-permute-start.17
  2817.9 12.4 collective-permute-start.18
  2821.9 10.5 collective-permute-start.19
  2824.2 10.1 collective-permute-start.20
  2828.4 12.5 collective-permute-start.22
  2830.3 12.7 collective-permute-start.10
  2832.4 28.6 collective-permute-start.11
  2834.3 28.6 collective-permute-start.2
  2836.3 29.2 collective-permute-start.3
  2840.8 26.7 collective-permute-start.4
  2843.0 26.5 collective-permute-start.5
  2861.0 11.1 collective-permute-start.6
  2862.9 11.5 collective-permute-start.7
  2865.5 12.7 collective-permute-start.8
  2867.6 12.7 collective-permute-start.9
  2869.5 20.1 collective-permute-start.34
  2872.1 20.2 collective-permute-start.24
  2874.5 20.9 collective-permute-start.25
  2878.2 19.1 collective-permute-start.26
  2881.0 18.3 collective-permute-start.27
  2889.7 14.3 collective-permute-start.28
  2892.3 24.5 collective-permute-start.29
  2895.4 21.3 collective-permute-start.30
  2897.3 27.4 collective-permute-start.31
  2899.3 25.4 collective-permute-start.32
  2904.0 20.8 collective-permute-start.33
  (118 other events, 9455.8 us)
Sparse Core Ops, SparseCore 0:
  11.0 76.4 all-gather.20
  90.6 72.6 all-gather.36
  1235.0 57.9 all-gather.30
  1296.2 62.0 all-gather.28
  1361.1 71.8 all-gather.18
  1435.9 92.2 all-gather.22
  1531.3 92.4 all-gather.24
  1626.9 92.4 all-gather.26
  1944.8 61.8 all-gather.32
  2009.9 62.0 all-gather.34
  2185.5 147.8 all-reduce.73
  2336.3 751.0 reduce-scatter.12
  3090.5 692.6 reduce-scatter.14
  3789.9 303.2 reduce-scatter.16
  4099.9 307.5 reduce-scatter.18
  4414.2 307.4 reduce-scatter.20
where the time goes:
time: 4760 us; the launch traced here: 4730 us
  waiting for transfers between devices  2160 us (45%)
  blocking collectives  1540 us (32%)
  local copies, waits for them, and re-layouts  417 us (9%)
  other arithmetic  254 us (5%)
  matrix products  238 us (5%)
  starting transfers between devices  106 us (2%)
    reduce_scatter x1, waiting for transfers between devices, body(): lax.psum_scatter(grad_input_weight, ('row', 'seq'), scatter_dimension=0,...  696 us
    unnamed x2, blocking collectives  562 us
    all_gather x1, blocking collectives, body(): lax.all_gather(shards[7], ('row', 'seq'), axis=0, tiled=True)  338 us
    all_gather x1, blocking collectives, body(): lax.all_gather(shards[5], ('row', 'seq'), axis=0, tiled=True)  321 us
    all_gather x1, blocking collectives, body(): lax.all_gather(shards[3], ('row', 'seq'), axis=0, tiled=True)  315 us
    reduce_scatter x1, waiting for transfers between devices, body(): lax.psum_scatter(grad_up_weight, ('row', 'seq'), scatter_dimension=0, til...  314 us
    reduce_scatter x1, waiting for transfers between devices, body(): lax.psum_scatter(grad_down_weight, ('row', 'seq'), scatter_dimension=0, t...  314 us
    reduce_scatter x1, waiting for transfers between devices, body(): lax.psum_scatter(grad_gate_weight, ('row', 'seq'), scatter_dimension=0, t...  310 us
  transfers between devices with their start and end apart: 51, of which 16 were waited for; matrix products, arithmetic and copies ran while one was open for 22% of the time, Pallas kernels for 0%

commit v1 on v0

v1 whole, which is shorter than its diff:
```python
from functools import partial

import jax
import jax.numpy as jnp
from jax import lax
from jax.experimental import pallas as pl
from jax.experimental.pallas import tpu as pltpu
from jax.sharding import Mesh
from jax.sharding import PartitionSpec as P

epsilon = 1e-06
beta_floor = 0.001
bf16 = jnp.bfloat16
f32 = jnp.float32
everywhere = ("row", "z", "y", "x")
team = ("row", "z")
plane = ("y", "x")
vmem_limit = 56 * 1024 * 1024


def hop(block, axis, distance):
    count = lax.axis_size(axis)
    return lax.ppermute(block, axis, [(i, (i + distance) % count) for i in range(count)])


def place(buffer, piece, at, dim):
    return lax.dynamic_update_slice_in_dim(buffer, jnp.expand_dims(piece, dim), at, dim)


def gather_axis(piece, axis, dim):
    mine = lax.axis_index(axis)
    shape = piece.shape[:dim] + (4,) + piece.shape[dim:]
    above, below, across = hop(piece, axis, -1), hop(piece, axis, 1), hop(piece, axis, 2)
    whole = place(jnp.zeros(shape, piece.dtype), piece, mine, dim)
    whole = place(whole, above, (mine + 1) % 4, dim)
    whole = place(whole, below, (mine + 3) % 4, dim)
    return place(whole, across, (mine + 2) % 4, dim)


def reduce_axis(whole, axis, dim):
    mine = lax.axis_index(axis)

    def piece(offset):
        return lax.dynamic_index_in_dim(whole, (mine + offset) % 4, dim, keepdims=False)

    total = piece(0).astype(f32)
    for offset in (2, 1, 3):
        total = total + hop(piece(offset).astype(bf16), axis, offset).astype(f32)
    return total


def gather_team(block):
    half = block.shape[0] // 2
    below, above = hop(block, "z", 1), hop(block, "z", -1)
    across = jnp.concatenate([hop(below[:half], "z", 1), hop(above[half:], "z", -1)], axis=0)
    parts = []
    for part in (block, above, across, below):
        parts += [part, hop(part, "row", 1)]
    return parts


def reduce_team(partial_sum):
    blocks = partial_sum.reshape(4, 2, -1, partial_sum.shape[-1])
    sums = [None] * 4
    for offset in (2, 1, 3, 0):
        sums[offset] = blocks[offset, 0].astype(f32) + hop(blocks[offset, 1].astype(bf16), "row", 1).astype(f32)
    half = sums[0].shape[0] // 2
    from_below = hop(sums[2][:half].astype(bf16), "z", 1)
    from_above = hop(sums[2][half:].astype(bf16), "z", -1)
    up = jnp.concatenate([sums[1][:half] + from_below.astype(f32), sums[1][half:]], axis=0)
    down = jnp.concatenate([sums[3][:half], sums[3][half:] + from_above.astype(f32)], axis=0)
    return (
        sums[0]
        + hop(up.astype(bf16), "z", 1).astype(f32)
        + hop(down.astype(bf16), "z", -1).astype(f32)
    )


def project_in(left, weight):
    return jnp.dot(left, weight, preferred_element_type=f32)


def project_back(grad, weight):
    return lax.dot_general(grad, weight, (((1,), (1,)), ((), ())), preferred_element_type=f32)


def outer_sum(left, grad):
    return lax.dot_general(left, grad, (((0,), (0,)), ((), ())), preferred_element_type=f32)


def kernel_call(kernel, outs, scratch=()):
    return pl.pallas_call(
        kernel,
        out_shape=[jax.ShapeDtypeStruct(shape, dtype) for shape, dtype in outs],
        scratch_shapes=list(scratch),
        compiler_params=pltpu.CompilerParams(vmem_limit_bytes=vmem_limit),
    )


def chunk_rows(chunk, size):
    return pl.ds(pl.multiple_of(chunk * size, size), size)


def panels(ref, rows):
    return jnp.concatenate([ref[at, rows, :] for at in range(ref.shape[0])], axis=1)


def set_panels(ref, rows, value):
    for at in range(ref.shape[0]):
        ref[at, rows, :] = value[:, at * 128 : (at + 1) * 128]


def gates_kernel(
    cin, halo, masks, params, w_in, w_rec,
    conv, factor, g_in, g_rec, kept_out, state, decay, ends, ext, raw_in, raw_rec, drive,
):
    tokens, width = cin.shape
    count = halo.shape[0]
    size = tokens // count
    tiles = width // 128

    def convolve(chunk, carry):
        rows = chunk_rows(chunk, size)
        ext[0:8, :] = halo[chunk].astype(f32)
        ext[8 : 8 + size, :] = cin[rows, :].astype(f32)
        total = params[4:5, :] + params[0:1, :] * ext[8 : 8 + size, :]
        for k in (1, 2, 3):
            total = total + params[k : k + 1, :] * ext[8 - k : 8 - k + size, :] * masks[rows, k : k + 1]
        conv[rows, :] = total.astype(bf16)
        return carry

    lax.fori_loop(0, count, convolve, 0)
    raw_in[...] = jnp.dot(conv[...], w_in[...], preferred_element_type=f32)
    raw_rec[...] = jnp.dot(conv[...], w_rec[...], preferred_element_type=f32)

    def gate(chunk, carry):
        rows = chunk_rows(chunk, size)
        gate_in = jax.nn.sigmoid(raw_in[rows, :] + params[5:6, :])
        gate_rec = jax.nn.sigmoid(raw_rec[rows, :] + params[6:7, :])
        log_decay = gate_rec * params[7:8, :]
        base = jnp.exp(log_decay)
        kept = -jnp.tanh(log_decay) * (base * base + 1.0)
        scale = jnp.sqrt(jnp.maximum(kept, beta_floor))
        set_panels(factor, rows, base * masks[rows, 0:1])
        g_in[rows, :] = gate_in
        g_rec[rows, :] = gate_rec
        kept_out[rows, :] = kept
        set_panels(drive, rows, scale * gate_in * conv[rows, :].astype(f32))
        return carry

    lax.fori_loop(0, count, gate, 0)

    def scan(slot, carry):
        at = pl.ds(slot, count, stride=size)
        after = []
        for tile, (held, gone) in enumerate(carry):
            step = factor[tile, at, :]
            held = step * held + drive[tile, at, :]
            gone = step * gone
            state[tile, at, :] = held
            decay[tile, at, :] = gone
            after.append((held, gone))
        return tuple(after)

    first = pl.ds(0, count, stride=size)
    start = []
    for tile in range(tiles):
        zero = drive[tile, first, :] * 0.0
        start.append((zero, zero + 1.0))
    last = lax.fori_loop(0, size, scan, tuple(start))
    for tile, (held, gone) in enumerate(last):
        ends[0, :, tile * 128 : (tile + 1) * 128] = gone
        ends[1, :, tile * 128 : (tile + 1) * 128] = held


def carry_kernel(backward, spot, pieces, entering):
    z_at, mine = spot[0], spot[1]
    places = pieces.shape[0]
    order = range(places - 1, -1, -1) if backward else range(places)
    decay, state = pieces[order[0], 0], pieces[order[0], 1]
    here = jnp.where(mine == order[0], 1.0, 0.0)
    own_decay, own_state = jnp.zeros_like(decay) + here, jnp.zeros_like(state)
    for place_at in order[1:]:
        here = jnp.where(mine == place_at, 1.0, 0.0)
        own_decay = own_decay + decay * here
        own_state = own_state + state * here
        step = pieces[place_at, 0]
        state = step * state + pieces[place_at, 1]
        decay = step * decay
    held = jnp.zeros((4, decay.shape[1]), f32)
    for step in range(4):
        z = 3 - step if backward else step
        offset = lax.rem(z - z_at + 4, 4)
        own = jnp.zeros_like(held)
        following = jnp.zeros_like(held)
        for candidate in range(4):
            pick = jnp.where(offset == candidate, 1.0, 0.0)
            part = slice(candidate * 4, candidate * 4 + 4)
            own = own + pick * (own_decay[part] * held + own_state[part])
            following = following + pick * (decay[part] * held + state[part])
        for row in range(4):
            entering[offset * 4 + row] = own[row : row + 1]
        held = following


def gelu_parts(value):
    slope = 0.7978845608028654
    square = value * value
    inner = jnp.tanh(slope * (value + 0.044715 * value * square))
    half = 0.5 * (1.0 + inner)
    act = value * half
    grad = half + 0.5 * value * (1.0 - inner * inner) * slope * (1.0 + 3 * 0.044715 * square)
    return act, grad


def mix_kernel(pre, state, decay, entering, out_rows, rec_state, mixed, partial_sum):
    count = entering.shape[0]
    tokens, width = rec_state.shape
    size = tokens // count

    def mix(chunk, carry):
        rows = chunk_rows(chunk, size)
        full = panels(state, rows) + panels(decay, rows) * entering[chunk]
        rec_state[rows, :] = full
        mixed[rows, :] = (gelu_parts(pre[rows, :])[0] * full).astype(bf16)
        return carry

    lax.fori_loop(0, count, mix, 0)

    def project(block, carry):
        rows = chunk_rows(block, 128)
        partial_sum[rows, :] = jnp.dot(
            mixed[rows, :], out_rows[...], preferred_element_type=f32
        ).astype(bf16)
        return carry

    lax.fori_loop(0, tokens // 128, project, 0)


def unmix_kernel(
    grad_mixed, pre, rec_state, factor, grad_gelu, adjoint, reach, ends, grad_state
):
    tokens, width = rec_state.shape
    count = ends.shape[1]
    size = tokens // count
    tiles = width // 128

    def unmix(chunk, carry):
        rows = chunk_rows(chunk, size)
        act, slope = gelu_parts(pre[rows, :])
        grad = grad_mixed[rows, :]
        grad_gelu[rows, :] = (grad * rec_state[rows, :] * slope).astype(bf16)
        set_panels(grad_state, rows, grad * act)
        return carry

    lax.fori_loop(0, count, unmix, 0)

    def scan(step, carry):
        at = pl.ds(size - 1 - step, count, stride=size)
        after = []
        for tile, (held, gone, ahead) in enumerate(carry):
            held = ahead * held + grad_state[tile, at, :]
            gone = ahead * gone
            adjoint[tile, at, :] = held
            reach[tile, at, :] = gone
            after.append((held, gone, factor[tile, at, :]))
        return tuple(after)

    first = pl.ds(0, count, stride=size)
    start = []
    for tile in range(tiles):
        zero = factor[tile, first, :] * 0.0
        start.append((zero, zero + 1.0, zero + 1.0))
    last = lax.fori_loop(0, size, scan, tuple(start))
    for tile, (held, gone, ahead) in enumerate(last):
        ends[0, :, tile * 128 : (tile + 1) * 128] = ahead * gone
        ends[1, :, tile * 128 : (tile + 1) * 128] = ahead * held


def ungate_kernel(
    adjoint, reach, arriving, rec_state, entering, factor, g_in, g_rec, kept, conv, cin, halo, masks,
    params, w_in, w_rec, grad_in, grad_rec, grad_conv, sums, ext, direct,
):
    tokens, width = cin.shape
    count = halo.shape[0]
    size = tokens // count
    zero = params[0:8, :] * 0.0

    def fold(value):
        total = value[0:8]
        for at in range(8, size, 8):
            total = total + value[at : at + 8]
        return total

    def ungate(chunk, carry):
        sum_in, sum_rec, sum_decay = carry
        rows = chunk_rows(chunk, size)
        ext[7:8, :] = entering[chunk]
        ext[8 : 8 + size, :] = rec_state[rows, :]
        full = panels(adjoint, rows) + panels(reach, rows) * arriving[chunk]
        square = kept[rows, :]
        scale = jnp.sqrt(jnp.maximum(square, beta_floor))
        gate_in = g_in[rows, :]
        gate_rec = g_rec[rows, :]
        values = conv[rows, :].astype(f32)
        scaled = full * scale
        drive = full * gate_in * values
        slope = jnp.where(square > beta_floor, (1.0 - square) / scale, 0.0)
        grad_log = full * panels(factor, rows) * ext[7 : 7 + size, :] - slope * drive
        raw_in = scale * drive * (1.0 - gate_in)
        pulled = grad_log * gate_rec
        raw_rec = pulled * params[7:8, :] * (1.0 - gate_rec)
        grad_in[rows, :] = raw_in.astype(bf16)
        grad_rec[rows, :] = raw_rec.astype(bf16)
        direct[rows, :] = scaled * gate_in
        return (sum_in + fold(raw_in), sum_rec + fold(raw_rec), sum_decay + fold(pulled))

    sum_in, sum_rec, sum_decay = lax.fori_loop(0, count, ungate, (zero, zero, zero))
    back = (((1,), (1,)), ((), ()))
    direct[...] += lax.dot_general(grad_in[...], w_in[...], back, preferred_element_type=f32)
    direct[...] += lax.dot_general(grad_rec[...], w_rec[...], back, preferred_element_type=f32)

    def taps(chunk, carry):
        sum_bias, sum_taps = carry
        rows = chunk_rows(chunk, size)
        grad = direct[rows, :].astype(bf16)
        grad_conv[rows, :] = grad
        grad = grad.astype(f32)
        ext[0:8, :] = halo[chunk].astype(f32)
        ext[8 : 8 + size, :] = cin[rows, :].astype(f32)
        new_taps = [sum_taps[0] + fold(grad * ext[8 : 8 + size, :])]
        for k in (1, 2, 3):
            moved = ext[8 - k : 8 - k + size, :] * masks[rows, k : k + 1]
            new_taps.append(sum_taps[k] + fold(grad * moved))
        return (sum_bias + fold(grad), tuple(new_taps))

    sum_bias, sum_taps = lax.fori_loop(0, count, taps, (zero, (zero,) * 4))
    rows_out = sum_taps + (sum_bias, sum_in, sum_rec, sum_decay * params[8:9, :])
    for index, total in enumerate(rows_out):
        sums[index : index + 1, :] = jnp.sum(total, axis=0, keepdims=True)


def unconvolve_kernel(grad_conv, halo, masks, params, out, ext):
    tokens, width = grad_conv.shape
    count = halo.shape[0]
    size = tokens // count

    def spread(chunk, carry):
        rows = chunk_rows(chunk, size)
        ext[0:size, :] = grad_conv[rows, :].astype(f32)
        ext[size : size + 8, :] = halo[chunk].astype(f32)
        total = params[0:1, :] * ext[0:size, :]
        for k in (1, 2, 3):
            total = total + params[k : k + 1, :] * ext[k : k + size, :] * masks[rows, 3 + k : 4 + k]
        out[rows, :] = total.astype(bf16)
        return carry

    lax.fori_loop(0, count, spread, 0)


def body(
    tokens,
    lengths,
    norm_one,
    gelu_weight,
    input_weight,
    conv_weight,
    conv_bias,
    gate_input,
    bias_input,
    gate_recur,
    bias_recur,
    decay_param,
    out_weight,
    norm_two,
    gate_weight,
    up_weight,
    down_weight,
    cotangent,
):
    row_count, size, model = tokens.shape
    local = row_count * size
    block, hidden = gelu_weight.shape
    inner = gate_weight.shape[1]
    head = gate_input.shape[1]
    channels, units = hidden // 8, inner // 8
    strip = gate_input.shape[0]
    width = -(-channels // 128) * 128
    spare = width - channels
    z_at, y_at, x_at = (lax.axis_index(name) for name in ("z", "y", "x"))
    plane_at = y_at * 4 + x_at
    chunks = 16
    total_tokens = chunks * size
    flat = tokens.reshape(local, model)

    token_parts = gather_team(flat)
    team_tokens = jnp.concatenate(token_parts, axis=0)

    gains = jnp.stack([norm_one, norm_two], axis=1)
    gains = jnp.broadcast_to(
        jnp.pad(gains, ((0, 0), (0, spare - 2)))[:, None, :], (block, 8, spare)
    )
    first = jnp.concatenate(
        [
            gelu_weight.reshape(block, 8, channels),
            gains,
            input_weight.reshape(block, 8, channels),
            jnp.zeros_like(gains),
        ],
        axis=2,
    ).transpose(1, 0, 2)
    first = lax.all_to_all(first, team, 0, 0, tiled=True)
    first_width = first.shape[2]
    first = gather_axis(first, "x", 1)
    first = gather_axis(first.reshape(8, 4 * block, first_width), "y", 1)
    first = first.reshape(model, first_width)
    small = jnp.stack([conv_bias, bias_input, bias_recur, decay_param], axis=1)
    second = jnp.concatenate([out_weight, gate_input, gate_recur, conv_weight, small], axis=1)
    second = gather_axis(gather_axis(second, "y", 0), "x", 1).reshape(channels, -1)
    second = jnp.pad(second, ((0, spare), (0, 0)))
    third = jnp.concatenate(
        [gate_weight.reshape(block, 8, units), up_weight.reshape(block, 8, units)], axis=2
    ).transpose(1, 0, 2)
    third = lax.all_to_all(third, team, 0, 0, tiled=True)
    third = lax.all_gather(third, plane, axis=0, tiled=False)
    third = third.reshape(16, 8, block, 2 * units).transpose(1, 0, 2, 3).reshape(model, 2 * units)
    down = lax.all_gather(down_weight, plane, axis=0, tiled=True)

    gain_one = first[:, channels].astype(f32)[None, :]
    gain_two = first[:, channels + 1].astype(f32)[None, :]
    out_rows = second[:, :model]
    own_head = (jnp.arange(width)[:, None] // head) == (jnp.arange(width)[None, :] // head)

    def spread_heads(part):
        return jnp.where(own_head, jnp.concatenate([part, part, part], axis=1)[:, :width], 0)

    w_in = spread_heads(second[:, model : model + head])
    w_rec = spread_heads(second[:, model + head : model + 2 * head])
    rows_small = second[:, model + 2 * head :].astype(f32).T
    decay_row = rows_small[7:8]
    params = jnp.concatenate(
        [
            rows_small[:7],
            -8.0 * jax.nn.softplus(decay_row),
            -8.0 * jax.nn.sigmoid(decay_row),
            jnp.zeros((7, width), f32),
        ],
        axis=0,
    )

    lens = jnp.stack([lengths, hop(lengths, "row", 1)], axis=0)
    starts = jnp.cumsum(lens, axis=2) - lens
    chunk_z = (z_at + jnp.arange(4)) % 4
    first_slot = chunk_z * (16 * size) + plane_at * size

    def position(slot):
        live = (lens > 0)[None, :, :, None, :] & (starts[None, :, :, None, :] <= slot[..., None])
        origin = jnp.max(jnp.where(live, starts[None, :, :, None, :], 0), axis=-1)
        return slot - origin

    slots = first_slot[:, None, None, None] + jnp.arange(size)[None, None, None, :]
    slots = jnp.broadcast_to(slots, (4, 2, row_count, size))
    here = position(slots)
    columns = [here != 0] + [here >= k for k in (1, 2, 3)]
    for k in (1, 2, 3):
        ahead = slots + k
        columns.append((position(ahead) >= k) & (ahead < 64 * size))
    columns.append(jnp.zeros_like(columns[0]))
    masks = jnp.stack(columns, axis=-1).astype(f32).reshape(total_tokens, 8)
    row_total = jnp.sum(lengths, axis=1)
    own_slots = (z_at * 16 + plane_at) * size + jnp.arange(size)
    valid = (own_slots[None, :] < row_total[:, None]).astype(f32).reshape(local, 1)

    token_float = team_tokens.astype(f32)
    scale_one = lax.rsqrt(jnp.mean(token_float * token_float, axis=-1, keepdims=True) + epsilon)
    normed = (token_float * scale_one * gain_one).astype(bf16)
    conv_in = project_in(normed, first[:, width:]).astype(bf16)
    by_chunk = (chunks, size, width)
    halo = hop(conv_in.reshape(by_chunk)[:, size - 8 :], plane, 1)
    halo = jnp.where(plane_at == 0, jnp.roll(halo, 4, axis=0), halo)
    gelu_pre = project_in(normed, first[:, :width])
    wide = ((total_tokens, width), f32)
    narrow = ((total_tokens, width), bf16)
    paneled = ((width // 128, total_tokens, 128), f32)
    ends_shape = ((2, chunks, width), f32)
    extended = pltpu.VMEM((size + 8, width), f32)
    whole = pltpu.VMEM(*wide)
    folded = pltpu.VMEM(*paneled)
    conv_vals, factor, g_in, g_rec, kept, local_state, decay, ends = kernel_call(
        gates_kernel,
        [narrow, paneled, wide, wide, wide, paneled, paneled, ends_shape],
        [extended, whole, whole, folded],
    )(conv_in, halo, masks, params, w_in, w_rec)

    def carried(ends, backward):
        pieces = lax.all_to_all(jnp.broadcast_to(ends, (16,) + ends.shape), plane, 0, 0, tiled=True)
        spot = jnp.stack([z_at, plane_at]).astype(jnp.int32)
        return pl.pallas_call(
            partial(carry_kernel, backward),
            out_shape=jax.ShapeDtypeStruct((chunks, 1, width), f32),
            in_specs=[pl.BlockSpec(memory_space=pltpu.SMEM), pl.BlockSpec(memory_space=pltpu.VMEM)],
            out_specs=pl.BlockSpec(memory_space=pltpu.VMEM),
        )(spot, pieces)

    entering = carried(ends, False)
    rec_state, mixed, partial_middle = kernel_call(
        mix_kernel, [wide, narrow, ((total_tokens, model), bf16)]
    )(gelu_pre, local_state, decay, entering, out_rows)
    own_tokens = flat.astype(f32)
    middle = own_tokens + reduce_team(partial_middle)

    scale_two = lax.rsqrt(jnp.mean(middle * middle, axis=-1, keepdims=True) + epsilon)
    normed_two = (middle * scale_two * gain_two).astype(bf16)
    upstream = cotangent.reshape(local, model).astype(f32) * valid
    grad_down = jnp.concatenate(gather_team(upstream.astype(bf16)), axis=0)
    team_two = jnp.concatenate(gather_team(normed_two), axis=0)
    pre = project_in(team_two, third)
    gate_pre, up_pre = pre[:, :units], pre[:, units:]
    gate_act, gate_slope = gelu_parts(gate_pre)
    inner_act = (gate_act * up_pre).astype(bf16)
    grad_inner = project_back(grad_down, down)
    grad_pre = jnp.concatenate(
        [(grad_inner * up_pre * gate_slope).astype(bf16), (grad_inner * gate_act).astype(bf16)],
        axis=1,
    )
    grad_two = reduce_team(project_back(grad_pre, third))
    result = (middle + reduce_team(project_in(inner_act, down))) * valid
    output = result.reshape(row_count, size, model).astype(bf16)

    def to_owners(grad):
        width = grad.shape[1]
        grad = grad.astype(bf16).reshape(8, 16, block, width).transpose(1, 0, 2, 3)
        grad = grad.reshape(16 * 8 * block, width)
        grad = lax.psum_scatter(grad, plane, scatter_dimension=0, tiled=True)
        return grad.reshape(8, block, width)

    def back_to_rows(grad):
        return lax.all_to_all(grad, team, 0, 0, tiled=True).astype(f32).transpose(1, 0, 2)

    grad_third = to_owners(outer_sum(team_two, grad_pre))
    grad_down_weight = lax.psum_scatter(
        outer_sum(inner_act, grad_down).astype(bf16), plane, scatter_dimension=0, tiled=True
    ).astype(f32)
    grad_third = back_to_rows(grad_third)
    grad_gate_weight = grad_third[:, :, :units].reshape(block, inner)
    grad_up_weight = grad_third[:, :, units:].reshape(block, inner)

    def norm_back(values, scale, gain, grad):
        pulled = gain * grad
        mean = jnp.mean(pulled * values, axis=-1, keepdims=True)
        return scale * pulled - values * (scale * scale * scale * mean)

    def gain_grad(gain, pairs):
        total = sum(jnp.sum(weight.astype(f32) * grad, axis=1) for weight, grad in pairs)
        return total / gain.astype(f32)

    grad_norm_two = gain_grad(
        norm_two, [(gate_weight, grad_gate_weight), (up_weight, grad_up_weight)]
    )
    grad_middle = upstream + norm_back(middle, scale_two, gain_two, grad_two)
    grad_branch = jnp.concatenate(gather_team(grad_middle.astype(bf16)), axis=0)

    grad_mixed = project_back(grad_branch, out_rows)
    grad_gelu, adjoint, reach, ends = kernel_call(
        unmix_kernel, [narrow, paneled, paneled, ends_shape], [folded]
    )(grad_mixed, gelu_pre, rec_state, factor)
    arriving = carried(ends, True)
    grad_in, grad_rec, grad_conv, sums = kernel_call(
        ungate_kernel, [narrow, narrow, narrow, ((8, width), f32)], [extended, whole]
    )(
        adjoint, reach, arriving, rec_state, entering, factor, g_in, g_rec, kept, conv_vals, conv_in,
        halo, masks, params, w_in, w_rec,
    )
    ahead = hop(grad_conv.reshape(by_chunk)[:, :8], plane, -1)
    ahead = jnp.where(plane_at == 15, jnp.roll(ahead, -4, axis=0), ahead)
    (grad_conv_in,) = kernel_call(unconvolve_kernel, [narrow], [extended])(
        grad_conv, ahead, masks, params
    )

    def own_heads(grad):
        grad = jnp.where(own_head, grad, 0)[:channels]
        return grad[:, :head] + grad[:, head:channels]

    grad_second = jnp.concatenate(
        [
            outer_sum(mixed, grad_branch)[:channels],
            own_heads(outer_sum(conv_vals, grad_in)),
            own_heads(outer_sum(conv_vals, grad_rec)),
            sums.T[:channels],
        ],
        axis=1,
    )
    grad_second = grad_second.astype(bf16).reshape(4, 4, strip, -1)
    grad_second = reduce_axis(reduce_axis(grad_second, "x", 1), "y", 0)
    grad_out_weight = grad_second[:, :model]
    grad_gate_input = grad_second[:, model : model + head]
    grad_gate_recur = grad_second[:, model + head : model + 2 * head]
    grad_small = grad_second[:, model + 2 * head :]

    grad_pair = jnp.concatenate([grad_gelu, grad_conv_in], axis=1)
    grad_normed = reduce_team(project_back(grad_pair, first))
    grad_first = outer_sum(normed, grad_pair).astype(bf16).reshape(8, 4, 4 * block, 2 * width)
    grad_first = reduce_axis(grad_first, "y", 1).reshape(8, 4, block, 2 * width)
    grad_first = reduce_axis(grad_first, "x", 1)
    grad_first = back_to_rows(grad_first.astype(bf16))
    grad_gelu_weight = grad_first[:, :, :channels].reshape(block, hidden)
    grad_input_weight = grad_first[:, :, width : width + channels].reshape(block, hidden)
    grad_norm_one = gain_grad(
        norm_one, [(gelu_weight, grad_gelu_weight), (input_weight, grad_input_weight)]
    )
    own_scale = lax.rsqrt(jnp.mean(own_tokens * own_tokens, axis=-1, keepdims=True) + epsilon)
    grad_tokens = grad_middle + norm_back(own_tokens, own_scale, gain_one, grad_normed)
    return (
        output,
        grad_tokens.reshape(row_count, size, model),
        grad_norm_one,
        grad_gelu_weight,
        grad_input_weight,
        grad_small[:, :4],
        grad_small[:, 4],
        grad_gate_input,
        grad_small[:, 5],
        grad_gate_recur,
        grad_small[:, 6],
        grad_small[:, 7],
        grad_out_weight,
        grad_norm_two,
        grad_gate_weight,
        grad_up_weight,
        grad_down_weight,
    )


def solution(mesh):
    grid = Mesh(mesh.devices.reshape(2, 4, 4, 4), everywhere)
    slots = P("row", ("z", "y", "x"), None)
    line = P(everywhere)
    sheet = P(everywhere, None)
    return jax.shard_map(
        body,
        mesh=grid,
        in_specs=(
            slots, P("row", None), line, sheet, sheet, sheet, line, sheet, line, sheet, line, line,
            sheet, line, sheet, sheet, sheet, slots,
        ),
        out_specs=(
            slots, slots, line, sheet, sheet, sheet, line, sheet, line, sheet, line, line, sheet,
            line, sheet, sheet, sheet,
        ),
        check_vma=False,
    )
```

time: 4760 us -> 669 us (0.14)
  waiting for transfers between devices: 2160 us -> 203 us
  blocking collectives: 1540 us -> 0 us
  local copies, waits for them, and re-layouts: 417 us -> 102 us
  other arithmetic: 254 us -> 45.5 us
  matrix products: 238 us -> 87.5 us
  Pallas kernels: 0 us -> 57.7 us
    reduce_scatter x5 -> x2, waiting for transfers between devices: 1780 us -> 0.03 us  [the longest x1 0.02 us: to_owners(): grad = lax.psum_scatter(grad, plane, scatter_dimension=0, tiled=True)]
    all_gather x3 -> x0, blocking collectives: 974 us -> none  [the longest x1 338 us: body(): lax.all_gather(shards[7], ('row', 'seq'), axis=0, tiled=True)]
    unnamed x2 -> x0, blocking collectives: 562 us -> none
    all_gather x10 -> x2, waiting for transfers between devices: 366 us -> 0.01 us  [the longest x1 0.01 us: body(): third = lax.all_gather(third, plane, axis=0, tiled=False)]
    ppermute x2 -> x91, waiting for transfers between devices: 1.72 us -> 186 us  [hop(): lax.ppermute(block, axis, [(i, (i + distance) % count) for i in range(cou...]
    slice x81 -> x37, local copies, waits for them, and re-layouts: 194 us -> 16.1 us  [the longest x2 3.92 us: body(): out_rows = second[:, :model]]
    ppermute x2 -> x91, starting transfers between devices: 2.99 us -> 121 us  [hop(): lax.ppermute(block, axis, [(i, (i + distance) % count) for i in range(cou...]
    unnamed x34 -> x0, starting transfers between devices: 102 us -> none
  transfers between devices with their start and end apart: 51 -> 101, of which waited for: 16 -> 33; matrix products, arithmetic and copies ran while one was open for 22% -> 30% of each run, Pallas kernels for 0% -> 9%
where the time goes in v1:
time: 669 us; the launch traced here: 658 us
  waiting for transfers between devices  203 us (30%)
  starting transfers between devices  147 us (22%)
  local copies, waits for them, and re-layouts  102 us (15%)
  matrix products  87.5 us (13%)
  Pallas kernels  57.7 us (9%)
  other arithmetic  45.5 us (7%)
  between operations  15.5 us (2%)
    ppermute x91, waiting for transfers between devices, hop(): lax.ppermute(block, axis, [(i, (i + distance) % count) for i in range(cou...  186 us
    ppermute x91, starting transfers between devices, hop(): lax.ppermute(block, axis, [(i, (i + distance) % count) for i in range(cou...  121 us
    unnamed x113, local copies, waits for them, and re-layouts  43.6 us
    dot_general x4, matrix products, project_back(): lax.dot_general(grad, weight, (((1,), (1,)), ((), ())), preferred_element...  34.6 us
    dot_general x6, matrix products, outer_sum(): lax.dot_general(left, grad, (((0,), (0,)), ((), ())), preferred_element_t...  30.4 us
    dot_general x4, matrix products, project_in(): return jnp.dot(left, weight, preferred_element_type=f32)  22.5 us
    pallas_call x1, Pallas kernels, body(): kernel_call(gates_kernel, [narrow, paneled, wide, wide, wide, paneled, pa...  15.2 us
  transfers between devices with their start and end apart: 101, of which 33 were waited for; matrix products, arithmetic and copies ran while one was open for 30% of the time, Pallas kernels for 9%

profile of v1, /device:TPU:1, one launch (start us, length us, event | category | flops | bytes accessed | tf_op | source)
XLA Modules:
  0.0 658.1 jit_solution(7171870533107407819)
XLA Ops:
  12.2 3.8 collective-permute-start.18
  23.0 5.4 all-to-all-start.2
  40.7 3.7 all-to-all-start
  46.8 5.1 all-to-all-done
  54.5 5.4 collective-permute-done.8
  59.9 10.6 %collective-permute-done.9 = bf16[8,16,768]{2,1,0:T(8,128)(2,1)S(1)} collective-permute-done((bf16[8,16,768]{2,1,0:T(8,128)(2,1)S(1)}, bf16[8,16,768]{2,1,0:T(8,128)(2,1)S(1)}, u32[]{:S(2)}, u32[]{:S(2)}) %collective-permute-start.9) | collective-permute-done | bytes 196640 | tf_op jit(solution)/shard_map/ppermute | solution.py:23
  72.0 4.5 collective-permute-done.10
  89.1 24.7 %collective-permute-done.19 = bf16[4,22,2408]{2,1,0:T(8,128)(2,1)S(1)} collective-permute-done((bf16[4,22,2408]{2,1,0:T(8,128)(2,1)S(1)}, bf16[4,22,2408]{2,1,0:T(8,128)(2,1)S(1)}, u32[]{:S(2)}, u32[]{:S(2)}) %collective-permute-start.19) | collective-permute-done | bytes 423840 | tf_op jit(solution)/shard_map/ppermute | solution.py:23
  116.7 10.2 %collective-permute-start.2 = (bf16[128,2048]{1,0:T(8,128)(2,1)}, bf16[128,2048]{1,0:T(8,128)(2,1)}, u32[]{:S(2)}, u32[]{:S(2)}) collective-permute-start(bf16[128,2048]{1,0:T(8,128)(2,1)} %collective-permute-done.1), channel_id=1, source_target_pairs={{0,64},{64,0},{1,65},{65,1},{2,66},{66,2},{3,67},{67,3},{4,68},{68... | collective-permute-start | bytes 1572872 | tf_op jit(solution)/shard_map/ppermute | solution.py:23
  140.5 25.2 %collective-permute-done.11 = bf16[8,64,768]{2,1,0:T(8,128)(2,1)S(1)} collective-permute-done((bf16[8,64,768]{2,1,0:T(8,128)(2,1)S(1)}, bf16[8,64,768]{2,1,0:T(8,128)(2,1)S(1)}, u32[]{:S(2)}, u32[]{:S(2)}) %collective-permute-start.11) | collective-permute-done | bytes 786464 | tf_op jit(solution)/shard_map/ppermute | solution.py:23
  180.9 4.2 collective-permute-done.14
  187.4 15.2 %shard_map.305 = (bf16[1024,384]{1,0:T(8,128)(2,1)}, f32[3,1024,128]{2,1,0:T(8,128)}, f32[1024,384]{1,0:T(8,128)}, f32[1024,384]{1,0:T(8,128)}, f32[1024,384]{1,...) custom-call(bf16[1024,384]{1,0:T(8,128)(2,1)} %copy-done.11, ...), custom_call_target="tpu_custom_call" | custom-call | tf_op jit(solution)/shard_map/pallas_call | solution.py:489
  204.4 3.6 all-to-all-start.1
  212.0 6.2 fusion.6.pre
  223.6 9.7 %shard_map.307 = (f32[1024,384]{1,0:T(8,128)}, bf16[1024,384]{1,0:T(8,128)(2,1)}, bf16[1024,2048]{1,0:T(8,128)(2,1)}) custom-call(f32[1024,384]{1,0:T(8,128)} %fusion.6.pre, f32[3,1024,128]{2,1,0:T(8,128)} %get-tuple-element.36.state, f32[3,1024,128]{2,1,0:T(8,128)} %get-tuple-element.37.decay, f32[16,1,384]{2,1,0:T(1,128)} %shard_map.306.entering, ...), custom_call_target="tpu_custom_call" | custom-call | tf_op jit(solution)/shard_map/pallas_call | solution.py:506
  251.7 4.9 collective-permute-done.28
  256.7 7.7 %collective-permute-done.25 = bf16[64,2048]{1,0:T(8,128)(2,1)S(1)} collective-permute-done((bf16[64,2048]{1,0:T(8,128)(2,1)S(1)}, bf16[64,2048]{1,0:T(8,128)(2,1)S(1)}, u32[]{:S(2)}, u32[]{:S(2)}) %collective-permute-start.25) | collective-permute-done | bytes 262176 | tf_op jit(solution)/shard_map/ppermute | solution.py:23
  268.4 7.5 %collective-permute-done.29 = bf16[128,2048]{1,0:T(8,128)(2,1)S(1)} collective-permute-done((bf16[128,2048]{1,0:T(8,128)(2,1)S(1)}, bf16[128,2048]{1,0:T(8,128)(2,1)S(1)}, u32[]{:S(2)}, u32[]{:S(2)}) %collective-permute-start.29) | collective-permute-done | bytes 524320 | tf_op jit(solution)/shard_map/ppermute | solution.py:23
  295.2 4.5 collective-permute-start.37
  314.9 10.5 %fusion.95 = f32[1024,1536]{1,0:T(8,128)} fusion(bf16[1024,2048]{1,0:T(8,128)(2,1)} %constant_dynamic-update-slice_fusion.9, bf16[2048,1536]{1,0:T(8,128)(2,1)S(1)} %bitcast.341), kind=kOutput, calls=%fused_computation.317 | convolution fusion | flops 6442450944 | bytes 16777216 | tf_op jit(solution)/shard_map/dot_general | solution.py:80
  325.4 11.3 %multiply_convert_fusion.1 = (bf16[1024,768]{1,0:T(8,128)(2,1)S(1)}, bf16[1024,768]{1,0:T(8,128)(2,1)S(1)}, bf16[1024,768]{1,0:T(8,128)(2,1)}) fusion(f32[1024,1536]{1,0:T(8,128)} %fusion.95, bf16[1024,2048]{1,0:T(8,128)(2,1)} %constant_dynamic-update-slice_fusion.18, bf16[768,2048]{1,0:T(8,128)(2,1)} %all-gather.4.cloned.1.call-done), kind=kOutput, calls=%fused_computation.10 | convolution fusion | flops 3240099840 | bytes 18350080 | tf_op jit(solution)/shard_map/dot_general | solution.py:84
  336.7 9.6 %convolution_convert_fusion = bf16[2048,1536]{1,0:T(8,128)(2,1)S(1)} fusion(bf16[1024,2048]{1,0:T(8,128)(2,1)} %constant_dynamic-update-slice_fusion.9, bf16[1024,768]{1,0:T(8,128)(2,1)S(1)} %get-tuple-element.208, bf16[1024,768]{1,0:T(8,128)(2,1)S(1)} %get-tuple-element.207), kind=kOutput, calls=%fused_computation.5 | convolution fusion | flops 6451888128 | bytes 13631488 | tf_op jit(solution)/shard_map/dot_general | solution.py:88
  351.3 11.9 %fusion.93 = (bf16[4,2,128,2048]{3,2,1,0:T(8,128)(2,1)S(1)}, f32[4,2,128,2048]{3,2,1,0:T(8,128)}) fusion(bf16[4,2,128,1536]{3,2,1,0:T(8,128)(2,1)} %bitcast.354, bf16[2048,1536,1,1]{1,0,3,2:T(8,128)(2,1)} %bitcast.342), kind=kOutput, calls=%fused_computation.315 | convolution fusion | flops 6444548096 | bytes 22020096 | tf_op jit(solution)/shard_map/dot_general | solution.py:84
  377.2 4.8 collective-permute-done.60
  385.8 4.4 collective-permute-done.44
  394.0 7.4 %collective-permute-done.61 = bf16[128,2048]{1,0:T(8,128)(2,1)S(1)} collective-permute-done((bf16[128,2048]{1,0:T(8,128)(2,1)S(1)}, bf16[128,2048]{1,0:T(8,128)(2,1)S(1)}, u32[]{:S(2)}, u32[]{:S(2)}) %collective-permute-start.61) | collective-permute-done | bytes 524320 | tf_op jit(solution)/shard_map/ppermute | solution.py:23
  404.6 8.1 %collective-permute-done.45 = bf16[128,2048]{1,0:T(8,128)(2,1)S(1)} collective-permute-done((bf16[128,2048]{1,0:T(8,128)(2,1)S(1)}, bf16[128,2048]{1,0:T(8,128)(2,1)S(1)}, u32[]{:S(2)}, u32[]{:S(2)}) %collective-permute-start.45) | collective-permute-done | bytes 524320 | tf_op jit(solution)/shard_map/ppermute | solution.py:23
  421.9 4.3 collective-permute-start.62
  426.5 3.8 collective-permute-done.65
  433.1 5.4 collective-permute-start.69
  447.8 5.7 fusion.83.grad_mixed
  453.5 12.3 %shard_map.308 = (bf16[1024,384]{1,0:T(8,128)(2,1)}, f32[3,1024,128]{2,1,0:T(8,128)}, f32[3,1024,128]{2,1,0:T(8,128)}, f32[2,16,384]{2,1,0:T(8,128)}) custom-call(f32[1024,384]{1,0:T(8,128)} %fusion.83.grad_mixed, f32[1024,384]{1,0:T(8,128)} %fusion.6.pre, f32[1024,384]{1,0:T(8,128)} %get-tuple-element.40.rec_state, f32[3,1024,128]{2,1,0:T(8,128)} %get-tuple-element.41.factor), custom_call_target="tpu_custom_call" | custom-call | tf_op jit(solution)/shard_map/pallas_call | solution.py:564
  471.6 7.9 %convolution_convert_fusion.1 = bf16[768,2048]{1,0:T(8,128)(2,1)} fusion(bf16[1024,768]{1,0:T(8,128)(2,1)} %get-tuple-element.218, bf16[1024,2048]{1,0:T(8,128)(2,1)} %constant_dynamic-update-slice_fusion.18), kind=kOutput, calls=%fused_computation.6 | convolution fusion | flops 3222798336 | bytes 8912896 | tf_op jit(solution)/shard_map/dot_general | solution.py:88
  479.5 4.0 fusion.97
  488.8 12.6 %shard_map.310 = (bf16[1024,384]{1,0:T(8,128)(2,1)}, bf16[1024,384]{1,0:T(8,128)(2,1)}, bf16[1024,384]{1,0:T(8,128)(2,1)}, f32[8,384]{1,0:T(8,128)}) custom-call(f32[3,1024,128]{2,1,0:T(8,128)} %get-tuple-element.43.adjoint, f32[3,1024,128]{2,1,0:T(8,128)} %get-tuple-element.44.reach, f32[16,1,384]{2,1,0:T(1,128)} %shard_map.309.arriving, ...), custom_call_target="tpu_custom_call" | custom-call | tf_op jit(solution)/shard_map/pallas_call | solution.py:568
  518.2 4.2 shard_map.311
  522.4 5.4 convolution_convert_fusion.2
  531.7 5.7 fusion.94
  539.6 3.7 collective-permute-done.86
  548.6 3.9 collective-permute-done.88
  552.5 4.2 collective-permute-start.76
  556.7 17.8 %collective-permute-done.90 = bf16[22,2408]{1,0:T(8,128)(2,1)S(1)} collective-permute-done((bf16[22,2408]{1,0:T(8,128)(2,1)S(1)}, bf16[22,2408]{1,0:T(8,128)(2,1)S(1)}, u32[]{:S(2)}, u32[]{:S(2)}) %collective-permute-start.90) | collective-permute-done | bytes 105984 | tf_op jit(solution)/shard_map/ppermute | solution.py:23
  586.2 12.8 %collective-permute-done.80 = bf16[8,64,768]{2,1,0:T(8,128)(2,1)S(1)} collective-permute-done((bf16[8,64,768]{2,1,0:T(8,128)(2,1)}, bf16[8,64,768]{2,1,0:T(8,128)(2,1)S(1)}, u32[]{:S(2)}, u32[]{:S(2)}) %collective-permute-start.80) | collective-permute-done | bytes 786464 | tf_op jit(solution)/shard_map/ppermute | solution.py:23
  608.7 3.7 collective-permute-done.84
  613.4 5.9 all-to-all-start.4
  621.5 3.9 all-to-all-done.4
  629.3 7.0 %collective-permute-done.75 = bf16[128,2048]{1,0:T(8,128)(2,1)S(1)} collective-permute-done((bf16[128,2048]{1,0:T(8,128)(2,1)}, bf16[128,2048]{1,0:T(8,128)(2,1)S(1)}, u32[]{:S(2)}, u32[]{:S(2)}) %collective-permute-start.75) | collective-permute-done | bytes 524320 | tf_op jit(solution)/shard_map/ppermute | solution.py:23
  638.1 4.1 all-to-all-start.5
  (492 shorter events, 274.0 us)
Async XLA Ops:
  12.2 34.4 %collective-permute-start.18 = (bf16[22,2408]{1,0:T(8,128)(2,1)S(1)}, bf16[22,2408]{1,0:T(8,128)(2,1)S(1)}, u32[]{:S(2)}, u32[]{:S(2)}) collective-permute-start(bf16[22,2408]{1,0:T(8,128)(2,1)S(1)} %concatenate.118), channel_id=1, source_target_pairs={{0,8},{4,12},{8,0},{12,4},{1,9},{5,13},{9,1},{13,5},{2,10},{6,14},... | collective-permute-start | bytes 317864 | tf_op jit(solution)/shard_map/ppermute | solution.py:23
  16.0 29.1 %collective-permute-start.17 = (bf16[22,2408]{1,0:T(8,128)(2,1)S(1)}, bf16[22,2408]{1,0:T(8,128)(2,1)S(1)}, u32[]{:S(2)}, u32[]{:S(2)}) collective-permute-start(bf16[22,2408]{1,0:T(8,128)(2,1)S(1)} %concatenate.118), channel_id=1, source_target_pairs={{0,4},{4,8},{8,12},{12,0},{1,5},{5,9},{9,13},{13,1},{2,6},{6,10},{... | collective-permute-start | bytes 317864 | tf_op jit(solution)/shard_map/ppermute | solution.py:23
  16.4 23.6 %collective-permute-start.16 = (bf16[22,2408]{1,0:T(8,128)(2,1)S(1)}, bf16[22,2408]{1,0:T(8,128)(2,1)S(1)}, u32[]{:S(2)}, u32[]{:S(2)}) collective-permute-start(bf16[22,2408]{1,0:T(8,128)(2,1)S(1)} %concatenate.118), channel_id=1, source_target_pairs={{0,12},{4,0},{8,4},{12,8},{1,13},{5,1},{9,5},{13,9},{2,14},{6,2},{... | collective-permute-start | bytes 317864 | tf_op jit(solution)/shard_map/ppermute | solution.py:23
  18.7 17.5 %collective-permute-start.15 = (s32[2,4]{1,0:T(2,128)}, s32[2,4]{1,0:T(2,128)S(1)}, u32[]{:S(2)}, u32[]{:S(2)}) collective-permute-start(s32[2,4]{1,0:T(2,128)} %param.19), channel_id=1, source_target_pairs={{0,64},{64,0},{1,65},{65,1},{2,66},{66,2},{3,67},{67,3},{4,68},{68... | collective-permute-start | bytes 104 | tf_op jit(solution)/shard_map/ppermute | solution.py:23
  23.0 17.6 %all-to-all-start.2 = ((bf16[8,16,1536]{2,1,0:T(8,128)(2,1)}), bf16[8,16,1536]{2,1,0:T(8,128)(2,1)S(1)}, u32[]{:S(2)}, u32[]{:S(2)}) async-start(bf16[8,16,1536]{2,1,0:T(8,128)(2,1)} %copy.328), calls=%async_computation.2 | async-start | bytes 786432 | tf_op jit(solution)/shard_map/all_to_all | solution.py:424
  28.5 48.5 %collective-permute-start.3 = (bf16[128,2048]{1,0:T(8,128)(2,1)}, bf16[128,2048]{1,0:T(8,128)(2,1)}, u32[]{:S(2)}, u32[]{:S(2)}) collective-permute-start(bf16[128,2048]{1,0:T(8,128)(2,1)} %bitcast.336), channel_id=1, source_target_pairs={{0,16},{16,32},{32,48},{48,0},{1,17},{17,33},{33,49},{49,1},{2,18}... | collective-permute-start | bytes 1572872 | tf_op jit(solution)/shard_map/ppermute | solution.py:23
  36.2 44.7 %collective-permute-start.1 = (bf16[128,2048]{1,0:T(8,128)(2,1)S(1)}, bf16[128,2048]{1,0:T(8,128)(2,1)}, u32[]{:S(2)}, u32[]{:S(2)}) collective-permute-start(bf16[128,2048]{1,0:T(8,128)(2,1)S(1)} %bitcast.338), channel_id=1, source_target_pairs={{0,48},{16,0},{32,16},{48,32},{1,49},{17,1},{33,17},{49,33},{2,50}... | collective-permute-start | bytes 1572872 | tf_op jit(solution)/shard_map/ppermute | solution.py:23
  40.0 44.4 %collective-permute-start = (bf16[128,2048]{1,0:T(8,128)(2,1)S(1)}, bf16[128,2048]{1,0:T(8,128)(2,1)}, u32[]{:S(2)}, u32[]{:S(2)}) collective-permute-start(bf16[128,2048]{1,0:T(8,128)(2,1)S(1)} %bitcast.339), channel_id=1, source_target_pairs={{0,64},{64,0},{1,65},{65,1},{2,66},{66,2},{3,67},{67,3},{4,68},{68... | collective-permute-start | bytes 1572872 | tf_op jit(solution)/shard_map/ppermute | solution.py:23
  44.4 264.6 %all-gather.6.cloned.1.call-start = ((), (), s32[]{:S(2)}) async-start(), calls=%async_computation.11 | async-start | bytes 6684672 | tf_op jit(solution)/shard_map/all_gather | solution.py:425
  45.1 193.4 %collective-permute-start.49 = (bf16[128,2048]{1,0:T(8,128)(2,1)}, bf16[128,2048]{1,0:T(8,128)(2,1)}, u32[]{:S(2)}, u32[]{:S(2)}) collective-permute-start(bf16[128,2048]{1,0:T(8,128)(2,1)} %get-tuple-element.284), channel_id=1, source_target_pairs={{0,16},{16,32},{32,48},{48,0},{1,17},{17,33},{33,49},{49,1},{2,18}... | collective-permute-start | bytes 1572872 | tf_op jit(solution)/shard_map/ppermute | solution.py:23
  76.5 163.5 %collective-permute-start.47 = (bf16[128,2048]{1,0:T(8,128)(2,1)}, bf16[128,2048]{1,0:T(8,128)(2,1)}, u32[]{:S(2)}, u32[]{:S(2)}) collective-permute-start(bf16[128,2048]{1,0:T(8,128)(2,1)} %get-tuple-element.284), channel_id=1, source_target_pairs={{0,48},{16,0},{32,16},{48,32},{1,49},{17,1},{33,17},{49,33},{2,50}... | collective-permute-start | bytes 1572872 | tf_op jit(solution)/shard_map/ppermute | solution.py:23
  77.0 39.7 %collective-permute-start.21 = (bf16[4,22,2408]{2,1,0:T(8,128)(2,1)S(1)}, bf16[4,22,2408]{2,1,0:T(8,128)(2,1)S(1)}, u32[]{:S(2)}, u32[]{:S(2)}) collective-permute-start(bf16[4,22,2408]{2,1,0:T(8,128)(2,1)S(1)} %copy-done.19), channel_id=1, source_target_pairs={{0,2},{1,3},{2,0},{3,1},{4,6},{5,7},{6,4},{7,5},{8,10},{9,11},{10,... | collective-permute-start | bytes 1271432 | tf_op jit(solution)/shard_map/ppermute | solution.py:23
  80.9 35.3 %collective-permute-start.20 = (bf16[4,22,2408]{2,1,0:T(8,128)(2,1)S(1)}, bf16[4,22,2408]{2,1,0:T(8,128)(2,1)S(1)}, u32[]{:S(2)}, u32[]{:S(2)}) collective-permute-start(bf16[4,22,2408]{2,1,0:T(8,128)(2,1)S(1)} %copy-done.19), channel_id=1, source_target_pairs={{0,1},{1,2},{2,3},{3,0},{4,5},{5,6},{6,7},{7,4},{8,9},{9,10},{10,1... | collective-permute-start | bytes 1271432 | tf_op jit(solution)/shard_map/ppermute | solution.py:23
  84.5 29.4 %collective-permute-start.19 = (bf16[4,22,2408]{2,1,0:T(8,128)(2,1)S(1)}, bf16[4,22,2408]{2,1,0:T(8,128)(2,1)S(1)}, u32[]{:S(2)}, u32[]{:S(2)}) collective-permute-start(bf16[4,22,2408]{2,1,0:T(8,128)(2,1)S(1)} %copy-done.19), channel_id=1, source_target_pairs={{0,3},{1,0},{2,1},{3,2},{4,7},{5,4},{6,5},{7,6},{8,11},{9,8},{10,9... | collective-permute-start | bytes 1271432 | tf_op jit(solution)/shard_map/ppermute | solution.py:23
  113.8 18.6 %collective-permute-start.4 = (bf16[64,2048]{1,0:T(8,128)(2,1)}, bf16[64,2048]{1,0:T(8,128)(2,1)}, u32[]{:S(2)}, u32[]{:S(2)}) collective-permute-start(bf16[64,2048]{1,0:T(8,128)(2,1)} %slice.454), channel_id=1, source_target_pairs={{0,16},{16,32},{32,48},{48,0},{1,17},{17,33},{33,49},{49,1},{2,18}... | collective-permute-start | bytes 786440 | tf_op jit(solution)/shard_map/ppermute | solution.py:23
  116.7 17.5 %collective-permute-start.2 = (bf16[128,2048]{1,0:T(8,128)(2,1)}, bf16[128,2048]{1,0:T(8,128)(2,1)}, u32[]{:S(2)}, u32[]{:S(2)}) collective-permute-start(bf16[128,2048]{1,0:T(8,128)(2,1)} %collective-permute-done.1), channel_id=1, source_target_pairs={{0,64},{64,0},{1,65},{65,1},{2,66},{66,2},{3,67},{67,3},{4,68},{68... | collective-permute-start | bytes 1572872 | tf_op jit(solution)/shard_map/ppermute | solution.py:23
  132.4 38.4 %collective-permute-start.13 = (bf16[8,64,768]{2,1,0:T(8,128)(2,1)S(1)}, bf16[8,64,768]{2,1,0:T(8,128)(2,1)S(1)}, u32[]{:S(2)}, u32[]{:S(2)}) collective-permute-start(bf16[8,64,768]{2,1,0:T(8,128)(2,1)S(1)} %bitcast.356), channel_id=1, source_target_pairs={{0,8},{4,12},{8,0},{12,4},{1,9},{5,13},{9,1},{13,5},{2,10},{6,14},... | collective-permute-start | bytes 2359304 | tf_op jit(solution)/shard_map/ppermute | solution.py:23
  132.4 33.3 %collective-permute-start.11 = (bf16[8,64,768]{2,1,0:T(8,128)(2,1)S(1)}, bf16[8,64,768]{2,1,0:T(8,128)(2,1)S(1)}, u32[]{:S(2)}, u32[]{:S(2)}) collective-permute-start(bf16[8,64,768]{2,1,0:T(8,128)(2,1)S(1)} %bitcast.357), channel_id=1, source_target_pairs={{0,12},{4,0},{8,4},{12,8},{1,13},{5,1},{9,5},{13,9},{2,14},{6,2},{... | collective-permute-start | bytes 2359304 | tf_op jit(solution)/shard_map/ppermute | solution.py:23
  134.3 36.0 %collective-permute-start.12 = (bf16[8,64,768]{2,1,0:T(8,128)(2,1)S(1)}, bf16[8,64,768]{2,1,0:T(8,128)(2,1)S(1)}, u32[]{:S(2)}, u32[]{:S(2)}) collective-permute-start(bf16[8,64,768]{2,1,0:T(8,128)(2,1)S(1)} %bitcast.358), channel_id=1, source_target_pairs={{0,4},{4,8},{8,12},{12,0},{1,5},{5,9},{9,13},{13,1},{2,6},{6,10},{... | collective-permute-start | bytes 2359304 | tf_op jit(solution)/shard_map/ppermute | solution.py:23
  165.8 75.3 %collective-permute-start.46 = (bf16[128,2048]{1,0:T(8,128)(2,1)}, bf16[128,2048]{1,0:T(8,128)(2,1)}, u32[]{:S(2)}, u32[]{:S(2)}) collective-permute-start(bf16[128,2048]{1,0:T(8,128)(2,1)} %get-tuple-element.284), channel_id=1, source_target_pairs={{0,64},{64,0},{1,65},{65,1},{2,66},{66,2},{3,67},{67,3},{4,68},{68... | collective-permute-start | bytes 1572872 | tf_op jit(solution)/shard_map/ppermute | solution.py:23
  204.4 16.5 %all-to-all-start.1 = ((f32[16,2,16,384]{3,2,1,0:T(8,128)}), f32[16,2,16,384]{3,2,1,0:T(8,128)S(1)}, u32[]{:S(2)}, u32[]{:S(2)}) async-start(f32[16,2,16,384]{3,2,1,0:T(8,128)} %broadcast_in_dim.183), calls=%async_computation.1 | async-start | bytes 1572864 | tf_op jit(solution)/shard_map/all_to_all | solution.py:496
  208.0 117.4 %all-gather.4.cloned.1.call-start = ((), (), s32[]{:S(2)}) async-start(), calls=%async_computation.8 | async-start | bytes 3342336 | tf_op jit(solution)/shard_map/all_gather | solution.py:427
  239.0 399.0 %reduce-scatter.3.cloned.1.call-start = ((), (), s32[]{:S(2)}) async-start(), calls=%async_computation.9 | async-start | bytes 6684672 | tf_op jit(solution)/shard_map/reduce_scatter | solution.py:534
  246.0 43.8 %collective-permute-start.53 = (bf16[128,2048]{1,0:T(8,128)(2,1)}, bf16[128,2048]{1,0:T(8,128)(2,1)S(1)}, u32[]{:S(2)}, u32[]{:S(2)}) collective-permute-start(bf16[128,2048]{1,0:T(8,128)(2,1)} %collective-permute-done.49), channel_id=1, source_target_pairs={{0,64},{64,0},{1,65},{65,1},{2,66},{66,2},{3,67},{67,3},{4,68},{68... | collective-permute-start | bytes 1572872 | tf_op jit(solution)/shard_map/ppermute | solution.py:23
  246.6 19.0 %collective-permute-start.48 = (bf16[128,2048]{1,0:T(8,128)(2,1)}, bf16[128,2048]{1,0:T(8,128)(2,1)S(1)}, u32[]{:S(2)}, u32[]{:S(2)}) collective-permute-start(bf16[128,2048]{1,0:T(8,128)(2,1)} %collective-permute-done.47), channel_id=1, source_target_pairs={{0,64},{64,0},{1,65},{65,1},{2,66},{66,2},{3,67},{67,3},{4,68},{68... | collective-permute-start | bytes 1572872 | tf_op jit(solution)/shard_map/ppermute | solution.py:23
  250.9 36.0 %collective-permute-start.52 = (bf16[128,2048]{1,0:T(8,128)(2,1)S(1)}, bf16[128,2048]{1,0:T(8,128)(2,1)S(1)}, u32[]{:S(2)}, u32[]{:S(2)}) collective-permute-start(bf16[128,2048]{1,0:T(8,128)(2,1)S(1)} %pad_maximum_fusion.8), channel_id=1, source_target_pairs={{0,64},{64,0},{1,65},{65,1},{2,66},{66,2},{3,67},{67,3},{4,68},{68... | collective-permute-start | bytes 1572872 | tf_op jit(solution)/shard_map/ppermute | solution.py:23
  251.5 16.9 %collective-permute-start.22 = (bf16[128,2048]{1,0:T(8,128)(2,1)S(1)}, bf16[128,2048]{1,0:T(8,128)(2,1)S(1)}, u32[]{:S(2)}, u32[]{:S(2)}) collective-permute-start(bf16[128,2048]{1,0:T(8,128)(2,1)S(1)} %get-tuple-element.231), channel_id=1, source_target_pairs={{0,64},{64,0},{1,65},{65,1},{2,66},{66,2},{3,67},{67,3},{4,68},{68... | collective-permute-start | bytes 1572872 | tf_op jit(solution)/shard_map/ppermute | solution.py:23
  283.4 16.3 %collective-permute-start.30 = (bf16[128,2048]{1,0:T(8,128)(2,1)S(1)}, bf16[128,2048]{1,0:T(8,128)(2,1)S(1)}, u32[]{:S(2)}, u32[]{:S(2)}) collective-permute-start(bf16[128,2048]{1,0:T(8,128)(2,1)S(1)} %get-tuple-element.204), channel_id=1, source_target_pairs={{0,64},{64,0},{1,65},{65,1},{2,66},{66,2},{3,67},{67,3},{4,68},{68... | collective-permute-start | bytes 1572872 | tf_op jit(solution)/shard_map/ppermute | solution.py:23
  363.4 30.6 %collective-permute-start.54 = (bf16[128,2048]{1,0:T(8,128)(2,1)S(1)}, bf16[128,2048]{1,0:T(8,128)(2,1)S(1)}, u32[]{:S(2)}, u32[]{:S(2)}) collective-permute-start(bf16[128,2048]{1,0:T(8,128)(2,1)S(1)} %get-tuple-element.223), channel_id=1, source_target_pairs={{0,64},{64,0},{1,65},{65,1},{2,66},{66,2},{3,67},{67,3},{4,68},{68... | collective-permute-start | bytes 1572872 | tf_op jit(solution)/shard_map/ppermute | solution.py:23
  369.5 35.1 %collective-permute-start.38 = (bf16[128,2048]{1,0:T(8,128)(2,1)S(1)}, bf16[128,2048]{1,0:T(8,128)(2,1)S(1)}, u32[]{:S(2)}, u32[]{:S(2)}) collective-permute-start(bf16[128,2048]{1,0:T(8,128)(2,1)S(1)} %get-tuple-element.227), channel_id=1, source_target_pairs={{0,64},{64,0},{1,65},{65,1},{2,66},{66,2},{3,67},{67,3},{4,68},{68... | collective-permute-start | bytes 1572872 | tf_op jit(solution)/shard_map/ppermute | solution.py:23
  390.6 22.1 %collective-permute-start.45 = (bf16[128,2048]{1,0:T(8,128)(2,1)S(1)}, bf16[128,2048]{1,0:T(8,128)(2,1)S(1)}, u32[]{:S(2)}, u32[]{:S(2)}) collective-permute-start(bf16[128,2048]{1,0:T(8,128)(2,1)S(1)} %pad_maximum_fusion.7), channel_id=1, source_target_pairs={{0,48},{16,0},{32,16},{48,32},{1,49},{17,1},{33,17},{49,33},{2,50}... | collective-permute-start | bytes 1572872 | tf_op jit(solution)/shard_map/ppermute | solution.py:23
  393.9 20.1 %collective-permute-start.42 = (bf16[128,2048]{1,0:T(8,128)(2,1)S(1)}, bf16[128,2048]{1,0:T(8,128)(2,1)S(1)}, u32[]{:S(2)}, u32[]{:S(2)}) collective-permute-start(bf16[128,2048]{1,0:T(8,128)(2,1)S(1)} %pad_maximum_fusion.6), channel_id=1, source_target_pairs={{0,16},{16,32},{32,48},{48,0},{1,17},{17,33},{33,49},{49,1},{2,18}... | collective-permute-start | bytes 1572872 | tf_op jit(solution)/shard_map/ppermute | solution.py:23
  421.9 16.7 %collective-permute-start.62 = (bf16[128,2048]{1,0:T(8,128)(2,1)}, bf16[128,2048]{1,0:T(8,128)(2,1)}, u32[]{:S(2)}, u32[]{:S(2)}) collective-permute-start(bf16[128,2048]{1,0:T(8,128)(2,1)} %get-tuple-element.202), channel_id=1, source_target_pairs={{0,64},{64,0},{1,65},{65,1},{2,66},{66,2},{3,67},{67,3},{4,68},{68... | collective-permute-start | bytes 1572872 | tf_op jit(solution)/shard_map/ppermute | solution.py:23
  467.5 18.5 %all-to-all-start.3 = ((f32[16,2,16,384]{3,2,1,0:T(8,128)}), f32[16,2,16,384]{3,2,1,0:T(8,128)S(1)}, u32[]{:S(2)}, u32[]{:S(2)}) async-start(f32[16,2,16,384]{3,2,1,0:T(8,128)} %broadcast_in_dim.184), calls=%async_computation.3 | async-start | bytes 1572864 | tf_op jit(solution)/shard_map/all_to_all | solution.py:496
  471.1 173.8 %reduce-scatter.5.cloned.1.call-start = ((), (), s32[]{:S(2)}) async-start(), calls=%async_computation.10 | async-start | bytes 3342336 | tf_op jit(solution)/shard_map/reduce_scatter | solution.py:541
  515.9 21.6 %collective-permute-start.85 = (bf16[4,22,2408]{2,1,0:T(8,128)(2,1)}, bf16[4,22,2408]{2,1,0:T(8,128)(2,1)S(1)}, u32[]{:S(2)}, u32[]{:S(2)}) collective-permute-start(bf16[4,22,2408]{2,1,0:T(8,128)(2,1)} %get-tuple-element.241), channel_id=1, source_target_pairs={{0,2},{1,3},{2,0},{3,1},{4,6},{5,7},{6,4},{7,5},{8,10},{9,11},{10,... | collective-permute-start | bytes 1271432 | tf_op jit(solution)/shard_map/ppermute | solution.py:23
  515.9 23.7 %collective-permute-start.87 = (bf16[4,22,2408]{2,1,0:T(8,128)(2,1)}, bf16[4,22,2408]{2,1,0:T(8,128)(2,1)}, u32[]{:S(2)}, u32[]{:S(2)}) collective-permute-start(bf16[4,22,2408]{2,1,0:T(8,128)(2,1)} %get-tuple-element.242), channel_id=1, source_target_pairs={{0,3},{1,0},{2,1},{3,2},{4,7},{5,4},{6,5},{7,6},{8,11},{9,8},{10,9... | collective-permute-start | bytes 1271432 | tf_op jit(solution)/shard_map/ppermute | solution.py:23
  516.2 27.2 %collective-permute-start.86 = (bf16[4,22,2408]{2,1,0:T(8,128)(2,1)}, bf16[4,22,2408]{2,1,0:T(8,128)(2,1)}, u32[]{:S(2)}, u32[]{:S(2)}) collective-permute-start(bf16[4,22,2408]{2,1,0:T(8,128)(2,1)} %get-tuple-element.243), channel_id=1, source_target_pairs={{0,1},{1,2},{2,3},{3,0},{4,5},{5,6},{6,7},{7,4},{8,9},{9,10},{10,1... | collective-permute-start | bytes 1271432 | tf_op jit(solution)/shard_map/ppermute | solution.py:23
  529.5 53.3 %collective-permute-start.79 = (bf16[8,64,768]{2,1,0:T(8,128)(2,1)}, bf16[8,64,768]{2,1,0:T(8,128)(2,1)}, u32[]{:S(2)}, u32[]{:S(2)}) collective-permute-start(bf16[8,64,768]{2,1,0:T(8,128)(2,1)} %get-tuple-element.238), channel_id=1, source_target_pairs={{0,8},{4,12},{8,0},{12,4},{1,9},{5,13},{9,1},{13,5},{2,10},{6,14},... | collective-permute-start | bytes 2359304 | tf_op jit(solution)/shard_map/ppermute | solution.py:23
  530.6 55.5 %collective-permute-start.81 = (bf16[8,64,768]{2,1,0:T(8,128)(2,1)}, bf16[8,64,768]{2,1,0:T(8,128)(2,1)}, u32[]{:S(2)}, u32[]{:S(2)}) collective-permute-start(bf16[8,64,768]{2,1,0:T(8,128)(2,1)} %get-tuple-element.239), channel_id=1, source_target_pairs={{0,12},{4,0},{8,4},{12,8},{1,13},{5,1},{9,5},{13,9},{2,14},{6,2},{... | collective-permute-start | bytes 2359304 | tf_op jit(solution)/shard_map/ppermute | solution.py:23
  546.0 28.5 %collective-permute-start.90 = (bf16[22,2408]{1,0:T(8,128)(2,1)S(1)}, bf16[22,2408]{1,0:T(8,128)(2,1)S(1)}, u32[]{:S(2)}, u32[]{:S(2)}) collective-permute-start(bf16[22,2408]{1,0:T(8,128)(2,1)S(1)} %get-tuple-element.252), channel_id=1, source_target_pairs={{0,12},{4,0},{8,4},{12,8},{1,13},{5,1},{9,5},{13,9},{2,14},{6,2},{... | collective-permute-start | bytes 317864 | tf_op jit(solution)/shard_map/ppermute | solution.py:23
  546.8 29.0 %collective-permute-start.89 = (bf16[22,2408]{1,0:T(8,128)(2,1)S(1)}, bf16[22,2408]{1,0:T(8,128)(2,1)S(1)}, u32[]{:S(2)}, u32[]{:S(2)}) collective-permute-start(bf16[22,2408]{1,0:T(8,128)(2,1)S(1)} %get-tuple-element.253), channel_id=1, source_target_pairs={{0,4},{4,8},{8,12},{12,0},{1,5},{5,9},{9,13},{13,1},{2,6},{6,10},{... | collective-permute-start | bytes 317864 | tf_op jit(solution)/shard_map/ppermute | solution.py:23
  552.5 26.2 %collective-permute-start.76 = (bf16[128,2048]{1,0:T(8,128)(2,1)}, bf16[128,2048]{1,0:T(8,128)(2,1)S(1)}, u32[]{:S(2)}, u32[]{:S(2)}) collective-permute-start(bf16[128,2048]{1,0:T(8,128)(2,1)} %get-tuple-element.220), channel_id=1, source_target_pairs={{0,64},{64,0},{1,65},{65,1},{2,66},{66,2},{3,67},{67,3},{4,68},{68... | collective-permute-start | bytes 1572872 | tf_op jit(solution)/shard_map/ppermute | solution.py:23
  578.7 20.3 %collective-permute-start.80 = (bf16[8,64,768]{2,1,0:T(8,128)(2,1)}, bf16[8,64,768]{2,1,0:T(8,128)(2,1)S(1)}, u32[]{:S(2)}, u32[]{:S(2)}) collective-permute-start(bf16[8,64,768]{2,1,0:T(8,128)(2,1)} %get-tuple-element.240), channel_id=1, source_target_pairs={{0,4},{4,8},{8,12},{12,0},{1,5},{5,9},{9,13},{13,1},{2,6},{6,10},{... | collective-permute-start | bytes 2359304 | tf_op jit(solution)/shard_map/ppermute | solution.py:23
  579.5 49.8 %collective-permute-start.71 = (bf16[128,2048]{1,0:T(8,128)(2,1)}, bf16[128,2048]{1,0:T(8,128)(2,1)S(1)}, u32[]{:S(2)}, u32[]{:S(2)}) collective-permute-start(bf16[128,2048]{1,0:T(8,128)(2,1)} %get-tuple-element.219), channel_id=1, source_target_pairs={{0,64},{64,0},{1,65},{65,1},{2,66},{66,2},{3,67},{67,3},{4,68},{68... | collective-permute-start | bytes 1572872 | tf_op jit(solution)/shard_map/ppermute | solution.py:23
  582.7 23.0 %collective-permute-start.74 = (bf16[64,2048]{1,0:T(8,128)(2,1)S(1)}, bf16[64,2048]{1,0:T(8,128)(2,1)S(1)}, u32[]{:S(2)}, u32[]{:S(2)}) collective-permute-start(bf16[64,2048]{1,0:T(8,128)(2,1)S(1)} %get-tuple-element.256), channel_id=1, source_target_pairs={{0,16},{16,32},{32,48},{48,0},{1,17},{17,33},{33,49},{49,1},{2,18}... | collective-permute-start | bytes 786440 | tf_op jit(solution)/shard_map/ppermute | solution.py:23
  582.8 20.9 %collective-permute-start.77 = (bf16[64,2048]{1,0:T(8,128)(2,1)S(1)}, bf16[64,2048]{1,0:T(8,128)(2,1)S(1)}, u32[]{:S(2)}, u32[]{:S(2)}) collective-permute-start(bf16[64,2048]{1,0:T(8,128)(2,1)S(1)} %get-tuple-element.257), channel_id=1, source_target_pairs={{0,48},{16,0},{32,16},{48,32},{1,49},{17,1},{33,17},{49,33},{2,50}... | collective-permute-start | bytes 786440 | tf_op jit(solution)/shard_map/ppermute | solution.py:23
  605.7 23.6 %collective-permute-start.78 = (bf16[128,2048]{1,0:T(8,128)(2,1)}, bf16[128,2048]{1,0:T(8,128)(2,1)S(1)}, u32[]{:S(2)}, u32[]{:S(2)}) collective-permute-start(bf16[128,2048]{1,0:T(8,128)(2,1)} %pad_maximum_fusion.13), channel_id=1, source_target_pairs={{0,48},{16,0},{32,16},{48,32},{1,49},{17,1},{33,17},{49,33},{2,50}... | collective-permute-start | bytes 1572872 | tf_op jit(solution)/shard_map/ppermute | solution.py:23
  (92 other events, 1012.1 us)
Sparse Core Ops, SparseCore 0:
  47.9 80.0 all-gather.5
  239.1 43.0 all-gather.3
  351.4 77.6 reduce-scatter.2
  479.6 99.9 reduce-scatter.4

commit v2 on v1

v2 whole, which is shorter than its diff:
```python
from functools import partial

import jax
import jax.numpy as jnp
from jax import lax
from jax.experimental import pallas as pl
from jax.experimental.pallas import tpu as pltpu
from jax.sharding import Mesh
from jax.sharding import PartitionSpec as P

epsilon = 1e-06
beta_floor = 0.001
bf16 = jnp.bfloat16
f32 = jnp.float32
everywhere = ("row", "z", "y", "x")
team = ("row", "z")
plane = ("y", "x")
vmem_limit = 32 * 1024 * 1024


def hop(block, axis, distance):
    count = lax.axis_size(axis)
    return lax.ppermute(block, axis, [(i, (i + distance) % count) for i in range(count)])


def gather_plane(piece):
    return lax.all_to_all(jnp.broadcast_to(piece, (16,) + piece.shape), plane, 0, 0, tiled=True)


def total_of(pieces):
    return jnp.sum(pieces.astype(f32), axis=0)


def after(value, *others):
    return lax.optimization_barrier((value,) + others)[0]


def joined(*parts):
    return jnp.concatenate(parts, axis=0)


def gather_team(block):
    z_at = lax.axis_index("z")
    half = block.shape[0] // 2
    below, above = hop(block, "z", 1), hop(block, "z", -1)
    across = joined(hop(below[:half], "z", 1), hop(above[half:], "z", -1))
    own = jnp.zeros((4,) + block.shape, block.dtype)
    for offset, part in ((0, block), (1, above), (3, below), (2, across)):
        own = lax.dynamic_update_index_in_dim(own, part, (z_at + offset) % 4, 0)
    own = own.reshape(4 * block.shape[0], -1)
    return own, hop(own, "row", 1), (above, below)


def reduce_team(other, own):
    z_at = lax.axis_index("z")
    other = hop(other, "row", 1).reshape(4, -1, other.shape[-1])
    own = own.reshape(other.shape)

    def block(offset):
        at = (z_at + offset) % 4
        parts = [lax.dynamic_index_in_dim(whole, at, 0, keepdims=False) for whole in (own, other)]
        return parts[0].astype(f32) + parts[1].astype(f32)

    sums = {offset: block(offset) for offset in (2, 1, 3, 0)}
    half = own.shape[1] // 2
    from_below = hop(sums[2][:half].astype(bf16), "z", 1)
    from_above = hop(sums[2][half:].astype(bf16), "z", -1)
    up = joined(sums[1][:half] + from_below.astype(f32), sums[1][half:]).astype(bf16)
    down = joined(sums[3][:half], sums[3][half:] + from_above.astype(f32)).astype(bf16)
    total = sums[0] + hop(up, "z", 1).astype(f32) + hop(down, "z", -1).astype(f32)
    return total, up


def project_in(left, weight):
    return jnp.dot(left, weight, preferred_element_type=f32)


def project_back(grad, weight):
    return lax.dot_general(grad, weight, (((1,), (1,)), ((), ())), preferred_element_type=f32)


def outer_sum(left, grad):
    return lax.dot_general(left, grad, (((0,), (0,)), ((), ())), preferred_element_type=f32)


def fold_down(rows, width):
    over = rows.shape[-1] - width
    group = rows.shape[-2] * over // width
    tail = [rows[..., at : at + group, width:] for at in range(0, rows.shape[-2], group)]
    return jnp.concatenate([rows[..., :width], jnp.concatenate(tail, axis=-1)], axis=-2)


def unfold_down(rows, model):
    width = rows.shape[-1]
    over = model - width
    count = rows.shape[-2] * width // model
    tail = rows[..., count:, :]
    tail = [tail[..., at : at + over] for at in range(0, width, over)]
    return jnp.concatenate([rows[..., :count, :], jnp.concatenate(tail, axis=-2)], axis=-1)


def cost(micros):
    return pl.CostEstimate(flops=0, bytes_accessed=int(micros * 3.0e6), transcendentals=0)


def kernel_call(kernel, micros, outs, scratch=()):
    return pl.pallas_call(
        kernel,
        cost_estimate=cost(micros),
        out_shape=[jax.ShapeDtypeStruct(shape, dtype) for shape, dtype in outs],
        scratch_shapes=list(scratch),
        compiler_params=pltpu.CompilerParams(vmem_limit_bytes=vmem_limit),
    )


def chunk_rows(chunk, size):
    return pl.ds(pl.multiple_of(chunk * size, size), size)


def panels(ref, rows):
    return jnp.concatenate([ref[at, rows, :] for at in range(ref.shape[0])], axis=1)


def set_panels(ref, rows, value):
    for at in range(ref.shape[0]):
        ref[at, rows, :] = value[:, at * 128 : (at + 1) * 128]


def gates_kernel(
    cin, halo, masks, params, w_in, w_rec,
    conv, factor, g_in, g_rec, kept_out, state, decay, ends, ext, raw_in, raw_rec, drive,
):
    tokens, width = cin.shape
    count = halo.shape[0]
    size = tokens // count
    tiles = width // 128

    def convolve(chunk, carry):
        rows = chunk_rows(chunk, size)
        ext[0:8, :] = halo[chunk].astype(f32)
        ext[8 : 8 + size, :] = cin[rows, :].astype(f32)
        total = params[4:5, :] + params[0:1, :] * ext[8 : 8 + size, :]
        for k in (1, 2, 3):
            total = total + params[k : k + 1, :] * ext[8 - k : 8 - k + size, :] * masks[rows, k : k + 1]
        conv[rows, :] = total.astype(bf16)
        return carry

    lax.fori_loop(0, count, convolve, 0)
    raw_in[...] = jnp.dot(conv[...], w_in[...], preferred_element_type=f32)
    raw_rec[...] = jnp.dot(conv[...], w_rec[...], preferred_element_type=f32)

    def gate(chunk, carry):
        rows = chunk_rows(chunk, size)
        gate_in = jax.nn.sigmoid(raw_in[rows, :] + params[5:6, :])
        gate_rec = jax.nn.sigmoid(raw_rec[rows, :] + params[6:7, :])
        log_decay = gate_rec * params[7:8, :]
        base = jnp.exp(log_decay)
        kept = -jnp.tanh(log_decay) * (base * base + 1.0)
        scale = jnp.sqrt(jnp.maximum(kept, beta_floor))
        set_panels(factor, rows, base * masks[rows, 0:1])
        g_in[rows, :] = gate_in
        g_rec[rows, :] = gate_rec
        kept_out[rows, :] = kept
        set_panels(drive, rows, scale * gate_in * conv[rows, :].astype(f32))
        return carry

    lax.fori_loop(0, count, gate, 0)

    def scan(slot, carry):
        at = pl.ds(slot, count, stride=size)
        after = []
        for tile, (held, gone) in enumerate(carry):
            step = factor[tile, at, :]
            held = step * held + drive[tile, at, :]
            gone = step * gone
            state[tile, at, :] = held
            decay[tile, at, :] = gone
            after.append((held, gone))
        return tuple(after)

    first = pl.ds(0, count, stride=size)
    start = []
    for tile in range(tiles):
        zero = drive[tile, first, :] * 0.0
        start.append((zero, zero + 1.0))
    last = lax.fori_loop(0, size, scan, tuple(start))
    for tile, (held, gone) in enumerate(last):
        ends[0, :, tile * 128 : (tile + 1) * 128] = gone
        ends[1, :, tile * 128 : (tile + 1) * 128] = held


def carry_kernel(backward, spot, pieces, entering):
    mine = spot[0]
    places = pieces.shape[0]
    order = range(places - 1, -1, -1) if backward else range(places)
    decay, state = pieces[order[0], 0], pieces[order[0], 1]
    here = jnp.where(mine == order[0], 1.0, 0.0)
    own_decay, own_state = jnp.zeros_like(decay) + here, jnp.zeros_like(state)
    for place_at in order[1:]:
        here = jnp.where(mine == place_at, 1.0, 0.0)
        own_decay = own_decay + decay * here
        own_state = own_state + state * here
        step = pieces[place_at, 0]
        state = step * state + pieces[place_at, 1]
        decay = step * decay
    for row in range(2):
        held = jnp.zeros((2, decay.shape[1]), f32)
        for z in range(3, -1, -1) if backward else range(4):
            start = row * 8 + z * 2
            part = slice(start, start + 2)
            inside = own_decay[part] * held + own_state[part]
            held = decay[part] * held + state[part]
            for line in range(2):
                entering[start + line] = inside[line : line + 1]


def gelu_parts(value):
    slope = 0.7978845608028654
    square = value * value
    inner = jnp.tanh(slope * (value + 0.044715 * value * square))
    half = 0.5 * (1.0 + inner)
    act = value * half
    grad = half + 0.5 * value * (1.0 - inner * inner) * slope * (1.0 + 3 * 0.044715 * square)
    return act, grad


def mix_kernel(pre, state, decay, entering, out_rows, rec_state, mixed, partial_sum):
    count = entering.shape[0]
    tokens, width = rec_state.shape
    size = tokens // count

    def mix(chunk, carry):
        rows = chunk_rows(chunk, size)
        full = panels(state, rows) + panels(decay, rows) * entering[chunk]
        rec_state[rows, :] = full
        mixed[rows, :] = (gelu_parts(pre[rows, :])[0] * full).astype(bf16)
        return carry

    lax.fori_loop(0, count, mix, 0)
    partial_sum[...] = jnp.dot(
        mixed[...], out_rows[...], preferred_element_type=f32
    ).astype(bf16)


def unmix_kernel(
    mixed_own, mixed_other, pre_own, pre_other, rec_own, rec_other, factor,
    grad_gelu, adjoint, reach, ends, grad_state,
):
    half, width = rec_own.shape
    count = ends.shape[1]
    size = 2 * half // count
    tiles = width // 128

    def unmix(start, grad_mixed, pre, rec_state, chunk, carry):
        rows = chunk_rows(chunk, size)
        out = chunk_rows(chunk + start, size)
        act, slope = gelu_parts(pre[rows, :])
        grad = grad_mixed[rows, :]
        grad_gelu[out, :] = (grad * rec_state[rows, :] * slope).astype(bf16)
        set_panels(grad_state, out, grad * act)
        return carry

    lax.fori_loop(0, count // 2, partial(unmix, 0, mixed_own, pre_own, rec_own), 0)
    lax.fori_loop(0, count // 2, partial(unmix, count // 2, mixed_other, pre_other, rec_other), 0)

    def scan(step, carry):
        at = pl.ds(size - 1 - step, count, stride=size)
        after = []
        for tile, (held, gone, ahead) in enumerate(carry):
            held = ahead * held + grad_state[tile, at, :]
            gone = ahead * gone
            adjoint[tile, at, :] = held
            reach[tile, at, :] = gone
            after.append((held, gone, factor[tile, at, :]))
        return tuple(after)

    first = pl.ds(0, count, stride=size)
    start = []
    for tile in range(tiles):
        zero = factor[tile, first, :] * 0.0
        start.append((zero, zero + 1.0, zero + 1.0))
    last = lax.fori_loop(0, size, scan, tuple(start))
    for tile, (held, gone, ahead) in enumerate(last):
        ends[0, :, tile * 128 : (tile + 1) * 128] = ahead * gone
        ends[1, :, tile * 128 : (tile + 1) * 128] = ahead * held


def ungate_kernel(
    adjoint, reach, arriving, rec_own, rec_other, entering, factor, g_in, g_rec, kept, conv, cin,
    halo, masks, params, w_in, w_rec, grad_in, grad_rec, grad_conv, sums, ext, direct,
):
    tokens, width = cin.shape
    count = halo.shape[0]
    size = tokens // count
    zero = params[0:8, :] * 0.0

    def fold(value):
        total = value[0:8]
        for at in range(8, size, 8):
            total = total + value[at : at + 8]
        return total

    def ungate(start, rec_state, chunk, carry):
        sum_in, sum_rec, sum_decay = carry
        ext[8 : 8 + size, :] = rec_state[chunk_rows(chunk, size), :]
        chunk = chunk + start
        rows = chunk_rows(chunk, size)
        ext[7:8, :] = entering[chunk]
        full = panels(adjoint, rows) + panels(reach, rows) * arriving[chunk]
        square = kept[rows, :]
        scale = jnp.sqrt(jnp.maximum(square, beta_floor))
        gate_in = g_in[rows, :]
        gate_rec = g_rec[rows, :]
        values = conv[rows, :].astype(f32)
        scaled = full * scale
        drive = full * gate_in * values
        slope = jnp.where(square > beta_floor, (1.0 - square) / scale, 0.0)
        grad_log = full * panels(factor, rows) * ext[7 : 7 + size, :] - slope * drive
        raw_in = scale * drive * (1.0 - gate_in)
        pulled = grad_log * gate_rec
        raw_rec = pulled * params[7:8, :] * (1.0 - gate_rec)
        grad_in[rows, :] = raw_in.astype(bf16)
        grad_rec[rows, :] = raw_rec.astype(bf16)
        direct[rows, :] = scaled * gate_in
        return (sum_in + fold(raw_in), sum_rec + fold(raw_rec), sum_decay + fold(pulled))

    half = count // 2
    totals = lax.fori_loop(0, half, partial(ungate, 0, rec_own), (zero, zero, zero))
    sum_in, sum_rec, sum_decay = lax.fori_loop(0, half, partial(ungate, half, rec_other), totals)
    back = (((1,), (1,)), ((), ()))
    direct[...] += lax.dot_general(grad_in[...], w_in[...], back, preferred_element_type=f32)
    direct[...] += lax.dot_general(grad_rec[...], w_rec[...], back, preferred_element_type=f32)

    def taps(chunk, carry):
        sum_bias, sum_taps = carry
        rows = chunk_rows(chunk, size)
        grad = direct[rows, :].astype(bf16)
        grad_conv[rows, :] = grad
        grad = grad.astype(f32)
        ext[0:8, :] = halo[chunk].astype(f32)
        ext[8 : 8 + size, :] = cin[rows, :].astype(f32)
        new_taps = [sum_taps[0] + fold(grad * ext[8 : 8 + size, :])]
        for k in (1, 2, 3):
            moved = ext[8 - k : 8 - k + size, :] * masks[rows, k : k + 1]
            new_taps.append(sum_taps[k] + fold(grad * moved))
        return (sum_bias + fold(grad), tuple(new_taps))

    sum_bias, sum_taps = lax.fori_loop(0, count, taps, (zero, (zero,) * 4))
    rows_out = sum_taps + (sum_bias, sum_in, sum_rec, sum_decay * params[8:9, :])
    for index, total in enumerate(rows_out):
        sums[index : index + 1, :] = jnp.sum(total, axis=0, keepdims=True)


def unconvolve_kernel(grad_conv, halo, masks, params, out, ext):
    tokens, width = grad_conv.shape
    count = halo.shape[0]
    size = tokens // count

    def spread(chunk, carry):
        rows = chunk_rows(chunk, size)
        ext[0:size, :] = grad_conv[rows, :].astype(f32)
        ext[size : size + 8, :] = halo[chunk].astype(f32)
        total = params[0:1, :] * ext[0:size, :]
        for k in (1, 2, 3):
            total = total + params[k : k + 1, :] * ext[k : k + size, :] * masks[rows, 3 + k : 4 + k]
        out[rows, :] = total.astype(bf16)
        return carry

    lax.fori_loop(0, count, spread, 0)


def body(
    tokens,
    lengths,
    norm_one,
    gelu_weight,
    input_weight,
    conv_weight,
    conv_bias,
    gate_input,
    bias_input,
    gate_recur,
    bias_recur,
    decay_param,
    out_weight,
    norm_two,
    gate_weight,
    up_weight,
    down_weight,
    cotangent,
):
    row_count, size, model = tokens.shape
    local = row_count * size
    block, hidden = gelu_weight.shape
    inner = gate_weight.shape[1]
    head = gate_input.shape[1]
    channels, units = hidden // 8, inner // 8
    strip = gate_input.shape[0]
    width = -(-channels // 128) * 128
    spare = width - channels
    row_at, z_at, y_at, x_at = (lax.axis_index(name) for name in everywhere)
    plane_at = y_at * 4 + x_at
    chunks = 16
    total_tokens = chunks * size
    flat = tokens.reshape(local, model)

    row_total = jnp.sum(lengths, axis=1)
    own_slots = (z_at * 16 + plane_at) * size + jnp.arange(size)
    valid = (own_slots[None, :] < row_total[:, None]).astype(f32).reshape(local, 1)
    upstream = cotangent.reshape(local, model).astype(f32) * valid

    def team_rows(block):
        whole = lax.all_gather(block, team, axis=0, tiled=False).reshape(2, 4 * local, model)
        return [
            lax.dynamic_index_in_dim(whole, row_at ^ other, 0, keepdims=False) for other in (0, 1)
        ]

    tokens_own, tokens_other = team_rows(flat)

    gains = jnp.stack([norm_one, norm_two], axis=1)
    gains = jnp.broadcast_to(
        jnp.pad(gains, ((0, 0), (0, spare - 2)))[:, None, :], (block, 8, spare)
    )
    lead = jnp.concatenate([input_weight.reshape(block, 8, channels), gains], axis=2)
    lead = lead.transpose(1, 0, 2)[:, None]
    lead = jnp.broadcast_to(lead, (8, 16, block, width)).reshape(model, width)
    input_full = lax.all_to_all(lead, everywhere, 0, 0, tiled=True)
    third = jnp.concatenate(
        [
            gate_weight.reshape(block, 8, units),
            up_weight.reshape(block, 8, units),
            gelu_weight.reshape(block, 8, channels),
            jnp.zeros_like(gains),
        ],
        axis=2,
    ).transpose(1, 0, 2)
    third = lax.all_to_all(after(third, input_full), team, 0, 0, tiled=True).reshape(8 * block, -1)
    first, third = third[:, 2 * units :], third[:, : 2 * units]
    small = jnp.stack([conv_bias, bias_input, bias_recur, decay_param], axis=1)
    rest = jnp.concatenate([gate_input, gate_recur, conv_weight, small], axis=1)
    rest = jnp.pad(rest, ((0, 32 - strip), (0, width - rest.shape[1])))
    rest = gather_plane(after(rest, first))[:, :strip].reshape(channels, width)
    rest = jnp.pad(rest, ((0, spare), (0, 0)))

    def in_order(rows, count):
        rows = rows.reshape(16, count, block, rows.shape[-1])
        return rows.transpose(1, 0, 2, 3).reshape(count * 16 * block, rows.shape[-1])

    cuts = -(-model // width)
    out_pack = jnp.pad(out_weight, ((0, 32 - strip), (0, cuts * width - model)))
    out_pack = out_pack.reshape(32, cuts, width).transpose(1, 0, 2).reshape(cuts * 32, width)
    second = jnp.concatenate([first, out_pack], axis=0)
    second = lax.all_gather(second, plane, axis=0, tiled=False)
    gelu_full = in_order(second[:, : 8 * block], 8)
    out_rows = second[:, 8 * block :].reshape(16, cuts, 32, width)[:, :, :strip]
    out_rows = out_rows.transpose(0, 2, 1, 3).reshape(channels, cuts * width)[:, :model]
    out_rows = jnp.pad(out_rows, ((0, spare), (0, 0)))

    third = jnp.concatenate([third, fold_down(down_weight, 2 * units)], axis=0)
    third = lax.all_gather(third, plane, axis=0, tiled=False)
    down = unfold_down(third[:, 8 * block :], model).reshape(units, model)
    third = in_order(third[:, : 8 * block], 8)

    gain_one = input_full[:, channels].astype(f32)[None, :]
    gain_two = input_full[:, channels + 1].astype(f32)[None, :]
    own_head = (jnp.arange(width)[:, None] // head) == (jnp.arange(width)[None, :] // head)

    def spread_heads(part):
        return jnp.where(own_head, jnp.concatenate([part, part, part], axis=1)[:, :width], 0)

    w_in = spread_heads(rest[:, :head])
    w_rec = spread_heads(rest[:, head : 2 * head])
    rows_small = rest[:, 2 * head : 2 * head + 8].astype(f32).T
    decay_row = rows_small[7:8]
    params = jnp.concatenate(
        [
            rows_small[:7],
            -8.0 * jax.nn.softplus(decay_row),
            -8.0 * jax.nn.sigmoid(decay_row),
            jnp.zeros((7, width), f32),
        ],
        axis=0,
    )

    lens = jnp.stack([lengths, hop(lengths, "row", 1)], axis=0)
    starts = jnp.cumsum(lens, axis=2) - lens
    first_slot = jnp.arange(4) * (16 * size) + plane_at * size

    def position(slot):
        live = (lens > 0)[:, None, :, None, :] & (starts[:, None, :, None, :] <= slot[..., None])
        origin = jnp.max(jnp.where(live, starts[:, None, :, None, :], 0), axis=-1)
        return slot - origin

    slots = first_slot[None, :, None, None] + jnp.arange(size)[None, None, None, :]
    slots = jnp.broadcast_to(slots, (2, 4, row_count, size))
    here = position(slots)
    columns = [here != 0] + [here >= k for k in (1, 2, 3)]
    for k in (1, 2, 3):
        ahead = slots + k
        columns.append((position(ahead) >= k) & (ahead < 64 * size))
    columns.append(jnp.zeros_like(columns[0]))
    masks = jnp.stack(columns, axis=-1).astype(f32).reshape(total_tokens, 8)

    def rms_unit(values):
        return lax.rsqrt(jnp.mean(values * values, axis=-1, keepdims=True) + epsilon)

    def norm_half(values):
        values = values.astype(f32)
        return (values * rms_unit(values) * gain_one).astype(bf16)

    normed_own, normed_other = norm_half(tokens_own), norm_half(tokens_other)

    def turned(rim, shift):
        by_z = rim.reshape((2, 4, row_count) + rim.shape[1:])
        return jnp.roll(by_z, shift, axis=1).reshape(rim.shape)

    conv_in = jnp.concatenate(
        [project_in(half, input_full).astype(bf16) for half in (normed_own, normed_other)], axis=0
    )
    by_chunk = (chunks, size, width)
    halo = hop(conv_in.reshape(by_chunk)[:, size - 8 :], plane, 1)
    halo = jnp.where(plane_at == 0, turned(halo, 1), halo)
    wide = ((total_tokens, width), f32)
    narrow = ((total_tokens, width), bf16)
    paneled = ((width // 128, total_tokens, 128), f32)
    ends_shape = ((2, chunks, width), f32)
    extended = pltpu.VMEM((size + 8, width), f32)
    whole = pltpu.VMEM(*wide)
    folded = pltpu.VMEM(*paneled)
    conv_vals, factor, g_in, g_rec, kept, local_state, decay, ends = kernel_call(
        gates_kernel,
        60,
        [narrow, paneled, wide, wide, wide, paneled, paneled, ends_shape],
        [extended, whole, whole, folded],
    )(conv_in, halo, masks, params, w_in, w_rec)

    down_own, down_other = team_rows(after(upstream.astype(bf16), ends))

    def carried(ends, backward):
        pieces = lax.all_to_all(jnp.broadcast_to(ends, (16,) + ends.shape), plane, 0, 0, tiled=True)
        spot = plane_at.astype(jnp.int32).reshape(1)
        return pl.pallas_call(
            partial(carry_kernel, backward),
            cost_estimate=cost(1),
            out_shape=jax.ShapeDtypeStruct((chunks, 1, width), f32),
            in_specs=[pl.BlockSpec(memory_space=pltpu.SMEM), pl.BlockSpec(memory_space=pltpu.VMEM)],
            out_specs=pl.BlockSpec(memory_space=pltpu.VMEM),
        )(spot, pieces)

    entering = carried(ends, False)
    gelu_own, gelu_other = project_in(normed_own, gelu_full), project_in(normed_other, gelu_full)
    half = total_tokens // 2

    def mix(which, gelu_pre):
        rows = pl.BlockSpec((half, width), lambda i: (0, 0))
        folds = pl.BlockSpec((width // 128, half, 128), lambda i: (0, which, 0))
        return pl.pallas_call(
            mix_kernel,
            cost_estimate=cost(5),
            out_shape=[
                jax.ShapeDtypeStruct((half, width), f32),
                jax.ShapeDtypeStruct((half, width), bf16),
                jax.ShapeDtypeStruct((half, model), bf16),
            ],
            grid=(1,),
            in_specs=[
                rows,
                folds,
                folds,
                pl.BlockSpec((chunks // 2, 1, width), lambda i: (which, 0, 0)),
                pl.BlockSpec((width, model), lambda i: (0, 0)),
            ],
            out_specs=[
                pl.BlockSpec((half, width), lambda i: (0, 0)),
                pl.BlockSpec((half, width), lambda i: (0, 0)),
                pl.BlockSpec((half, model), lambda i: (0, 0)),
            ],
            compiler_params=pltpu.CompilerParams(vmem_limit_bytes=vmem_limit),
        )(gelu_pre, local_state, decay, entering, out_rows)

    other_state, other_mixed, other_middle = mix(1, gelu_other)
    own_state, own_mixed, own_middle = mix(0, gelu_own)
    mixed = jnp.concatenate([own_mixed, other_mixed], axis=0)
    own_tokens = flat.astype(f32)
    middle = own_tokens + reduce_team(other_middle, own_middle)[0]

    scale_two = rms_unit(middle)
    normed_two = (middle * scale_two * gain_two).astype(bf16)
    two_own, two_other, _ = gather_team(normed_two)

    def feed(values, grad_inner):
        pre = project_in(values, third)
        act, slope = gelu_parts(pre[:, :units])
        up = pre[:, units:]
        grad = [(grad_inner * up * slope).astype(bf16), (grad_inner * act).astype(bf16)]
        return (act * up).astype(bf16), jnp.concatenate(grad, axis=1)

    inner_own, pre_own = feed(two_own, project_back(down_own, down))
    inner_other, pre_other = feed(two_other, project_back(down_other, down))
    terms_other = project_back(pre_other, third).astype(bf16)
    terms_own = project_back(pre_own, third).astype(bf16)
    grad_two, _ = reduce_team(terms_other, terms_own)
    grad_down, inner_act = joined(down_own, down_other), joined(inner_own, inner_other)
    team_two, grad_pre = joined(two_own, two_other), joined(pre_own, pre_other)

    def by_owner(grad):
        grad = grad.astype(bf16).reshape(-1, 16, block, grad.shape[1]).transpose(1, 0, 2, 3)
        return grad.reshape(16, -1, grad.shape[-1])

    def back_to_rows(grad):
        grad = grad.astype(bf16).reshape(8, block, -1)
        return lax.all_to_all(grad, team, 0, 0, tiled=True).astype(f32).transpose(1, 0, 2)

    def norm_back(values, scale, gain, grad):
        pulled = gain * grad
        mean = jnp.mean(pulled * values, axis=-1, keepdims=True)
        return scale * pulled - values * (scale * scale * scale * mean)

    def gain_grad(gain, pairs):
        total = sum(jnp.sum(weight.astype(f32) * grad, axis=1) for weight, grad in pairs)
        return total / gain.astype(f32)

    grad_middle = upstream + norm_back(middle, scale_two, gain_two, grad_two)
    branch_own, branch_other, first_branch = gather_team(grad_middle.astype(bf16))
    grad_third = jnp.concatenate(
        [
            by_owner(after(outer_sum(team_two, grad_pre).astype(bf16), *first_branch)),
            fold_down(
                after(outer_sum(inner_act, grad_down).astype(bf16), *first_branch).reshape(
                    16, -1, model
                ),
                2 * units,
            ),
        ],
        axis=1,
    )
    share = grad_third.shape[1]
    grad_third = lax.psum_scatter(
        grad_third.reshape(16 * share, 2 * units), plane, scatter_dimension=0, tiled=True
    )
    grad_down_weight = unfold_down(grad_third[8 * block :], model).astype(f32)

    grad_gelu, adjoint, reach, ends = kernel_call(
        unmix_kernel, 100, [narrow, paneled, paneled, ends_shape], [folded]
    )(
        project_back(branch_own, out_rows), project_back(branch_other, out_rows),
        gelu_own, gelu_other, own_state, other_state, factor,
    )
    normed = joined(normed_own, normed_other)
    grad_branch = joined(branch_own, branch_other)
    grad_out_weight = outer_sum(mixed, grad_branch)[:channels].astype(bf16)
    grad_gelu_full = outer_sum(normed, grad_gelu).astype(bf16)
    grad_out_rows = after(grad_out_weight, branch_other).reshape(16, strip, model)
    grad_out_rows = lax.all_to_all(grad_out_rows, plane, 0, 0, tiled=True)
    arriving = carried(after(ends, grad_out_rows), True)
    arriving = after(arriving, grad_gelu_full)
    grad_gelu_rows = after(by_owner(grad_gelu_full), arriving)
    grad_gelu_rows = lax.all_to_all(grad_gelu_rows, plane, 0, 0, tiled=True)
    grad_in, grad_rec, grad_conv, sums = kernel_call(
        ungate_kernel, 100, [narrow, narrow, narrow, ((8, width), f32)], [extended, whole]
    )(
        adjoint, reach, arriving, own_state, other_state, entering, factor, g_in, g_rec, kept,
        conv_vals, conv_in, halo, masks, params, w_in, w_rec,
    )
    first_half = lax.select(row_at == 0, inner_own, inner_other)
    inner_rows = joined(first_half, lax.select(row_at == 0, inner_other, inner_own))
    result = project_in(after(inner_rows, grad_conv), down).astype(bf16)
    result = lax.psum_scatter(result, team, scatter_dimension=0, tiled=True)
    result = (middle + result.astype(f32)) * valid
    output = result.reshape(row_count, size, model).astype(bf16)
    ahead = hop(grad_conv.reshape(by_chunk)[:, :8], plane, -1)
    ahead = jnp.where(plane_at == 15, turned(ahead, -1), ahead)
    (grad_conv_in,) = kernel_call(unconvolve_kernel, 1, [narrow], [extended])(
        grad_conv, ahead, masks, params
    )

    def own_heads(grad):
        grad = jnp.where(own_head, grad, 0)[:channels]
        return grad[:, :head] + grad[:, head:channels]

    grad_conv_in = after(grad_conv_in, grad_gelu_rows)
    grad_pair = jnp.concatenate([grad_conv_in, grad_gelu], axis=1)
    pair_weight = jnp.concatenate([input_full, gelu_full], axis=1)
    terms_other = project_back(grad_pair[half:], pair_weight).astype(bf16)
    grad_normed, upward = reduce_team(terms_other, project_back(grad_pair[:half], pair_weight).astype(bf16))
    grad_rest = jnp.concatenate(
        [
            own_heads(outer_sum(conv_vals, grad_in)),
            own_heads(outer_sum(conv_vals, grad_rec)),
            sums.T[:channels],
        ],
        axis=1,
    ).astype(bf16)
    grad_rest = grad_rest.reshape(16, strip, -1)
    grad_rest = jnp.pad(
        grad_rest, ((0, 0), (0, 32 - strip), (0, width - grad_rest.shape[2]))
    )
    grad_input_full = outer_sum(normed, grad_conv_in).astype(bf16)
    grad_lead = jnp.concatenate([by_owner(grad_input_full), grad_rest], axis=1)
    grad_lead = lax.all_to_all(grad_lead, plane, 0, 0, tiled=True)
    grad_lead = total_of(after(grad_lead, upward))
    cut = 8 * block
    grad_rest = grad_lead[cut : cut + strip]
    grad_out_weight = total_of(after(grad_out_rows, upward))
    grad_gelu_rows = total_of(after(grad_gelu_rows, upward)).astype(bf16)
    grad_gate_input = grad_rest[:, :head]
    grad_gate_recur = grad_rest[:, head : 2 * head]
    grad_small = grad_rest[:, 2 * head : 2 * head + 8]
    team_third = jnp.concatenate(
        [after(grad_third[:cut], upward), grad_lead[:cut].astype(bf16), grad_gelu_rows], axis=1
    )
    team_third = back_to_rows(team_third)
    grad_input_weight = team_third[:, :, 2 * units : 2 * units + channels].reshape(block, hidden)
    grad_gelu_weight = team_third[:, :, 2 * units + width :][:, :, :channels].reshape(block, hidden)
    grad_gate_weight = team_third[:, :, :units].reshape(block, inner)
    grad_up_weight = team_third[:, :, units : 2 * units].reshape(block, inner)

    grad_norm_two = gain_grad(
        norm_two, [(gate_weight, grad_gate_weight), (up_weight, grad_up_weight)]
    )
    grad_norm_one = gain_grad(
        norm_one, [(gelu_weight, grad_gelu_weight), (input_weight, grad_input_weight)]
    )
    own_scale = rms_unit(own_tokens)
    grad_tokens = grad_middle + norm_back(own_tokens, own_scale, gain_one, grad_normed)
    return (
        output,
        grad_tokens.reshape(row_count, size, model),
        grad_norm_one,
        grad_gelu_weight,
        grad_input_weight,
        grad_small[:, :4],
        grad_small[:, 4],
        grad_gate_input,
        grad_small[:, 5],
        grad_gate_recur,
        grad_small[:, 6],
        grad_small[:, 7],
        grad_out_weight,
        grad_norm_two,
        grad_gate_weight,
        grad_up_weight,
        grad_down_weight,
    )


def solution(mesh):
    grid = Mesh(mesh.devices.reshape(2, 4, 4, 4), everywhere)
    slots = P("row", ("z", "y", "x"), None)
    line = P(everywhere)
    sheet = P(everywhere, None)
    return jax.shard_map(
        body,
        mesh=grid,
        in_specs=(
            slots, P("row", None), line, sheet, sheet, sheet, line, sheet, line, sheet, line, line,
            sheet, line, sheet, sheet, sheet, slots,
        ),
        out_specs=(
            slots, slots, line, sheet, sheet, sheet, line, sheet, line, sheet, line, line, sheet,
            line, sheet, sheet, sheet,
        ),
        check_vma=False,
    )
```

time: 669 us -> 561 us (0.84)
  starting transfers between devices: 147 us -> 105 us
  waiting for transfers between devices: 203 us -> 162 us
  Pallas kernels: 57.7 us -> 34.2 us
  local copies, waits for them, and re-layouts: 102 us -> 80 us
  other arithmetic: 45.5 us -> 62.6 us
  blocking collectives: 0 us -> 15 us
  matrix products: 87.5 us -> 75.3 us
    ppermute x91 -> x28, waiting for transfers between devices: 186 us -> 78.4 us  [hop(): lax.ppermute(block, axis, [(i, (i + distance) % count) for i in range(cou...]
    ppermute x91 -> x28, starting transfers between devices: 121 us -> 56.8 us  [hop(): lax.ppermute(block, axis, [(i, (i + distance) % count) for i in range(cou...]
    all_to_all x2 -> x6, waiting for transfers between devices: 5.09 us -> 66.3 us  [the longest x1 22.8 us: body(): input_full = lax.all_to_all(lead, everywhere, 0, 0, tiled=True)]
    all_to_all x2 -> x6, starting transfers between devices: 9.1 us -> 36 us  [the longest x1 11.5 us: body(): input_full = lax.all_to_all(lead, everywhere, 0, 0, tiled=True)]
    pallas_call x7 -> x8, Pallas kernels: 57.7 us -> 34.2 us  [the longest x1 9.73 us: body(): kernel_call(gates_kernel, 60, [narrow, paneled, wide, wide, wide, paneled...]
    all_to_all x0 -> x1, blocking collectives: none -> 15 us  [carried(): lax.all_to_all(jnp.broadcast_to(ends, (16,) + ends.shape), plane, 0, 0, t...]
    concatenate x14 -> x17, other arithmetic: 5.15 us -> 19.4 us  [the longest x1 9.53 us: body(): jnp.concatenate([by_owner(after(outer_sum(team_two, grad_pre).astype(bf16...]
    unnamed x113 -> x242, local copies, waits for them, and re-layouts: 43.6 us -> 33.1 us
  transfers between devices with their start and end apart: 101 -> 42, of which waited for: 33 -> 24; matrix products, arithmetic and copies ran while one was open for 30% -> 28% of each run, Pallas kernels for 9% -> 6%
where the time goes in v2:
time: 561 us; the launch traced here: 551 us
  waiting for transfers between devices  162 us (29%)
  starting transfers between devices  105 us (19%)
  local copies, waits for them, and re-layouts  80 us (14%)
  matrix products  75.3 us (13%)
  other arithmetic  62.6 us (11%)
  Pallas kernels  34.2 us (6%)
  between operations  16.7 us (3%)
  blocking collectives  15 us (3%)
    ppermute x28, waiting for transfers between devices, hop(): lax.ppermute(block, axis, [(i, (i + distance) % count) for i in range(cou...  78.4 us
    ppermute x28, starting transfers between devices, hop(): lax.ppermute(block, axis, [(i, (i + distance) % count) for i in range(cou...  56.8 us
    unnamed x242, local copies, waits for them, and re-layouts  33.1 us
    dot_general x7, matrix products, outer_sum(): lax.dot_general(left, grad, (((0,), (0,)), ((), ())), preferred_element_t...  26.7 us
    dot_general x8, matrix products, project_back(): lax.dot_general(grad, weight, (((1,), (1,)), ((), ())), preferred_element...  25.1 us
    dot_general x7, matrix products, project_in(): return jnp.dot(left, weight, preferred_element_type=f32)  23.5 us
    all_to_all x1, waiting for transfers between devices, body(): input_full = lax.all_to_all(lead, everywhere, 0, 0, tiled=True)  22.8 us
    all_to_all x1, waiting for transfers between devices, body(): grad_out_rows = lax.all_to_all(grad_out_rows, plane, 0, 0, tiled=True)  15.6 us
  transfers between devices with their start and end apart: 42, of which 24 were waited for; matrix products, arithmetic and copies ran while one was open for 28% of the time, Pallas kernels for 6%

profile of v2, /device:TPU:1, one launch (start us, length us, event | category | flops | bytes accessed | tf_op | source)
XLA Modules:
  0.0 551.1 jit_solution(12425276060690897234)
XLA Ops:
  11.2 11.5 %all-to-all-start = ((bf16[128,16,384]{2,1,0:T(8,128)(2,1)}), bf16[128,16,384]{2,1,0:T(8,128)(2,1)S(1)}, u32[]{:S(2)}, u32[]{:S(2)}) async-start(bf16[128,16,384]{2,1,0:T(8,128)(2,1)} %bitcast.7), calls=%async_computation | async-start | bytes 3145728 | tf_op jit(solution)/shard_map/all_to_all | solution.py:427
  23.3 22.8 %all-to-all-done = bf16[128,16,384]{2,1,0:T(8,128)(2,1)S(1)} async-done(((bf16[128,16,384]{2,1,0:T(8,128)(2,1)}), bf16[128,16,384]{2,1,0:T(8,128)(2,1)S(1)}, u32[]{:S(2)}, u32[]{:S(2)}) %all-to-all-start) | async-done | bytes 1572896 | tf_op jit(solution)/shard_map/all_to_all | solution.py:427
  47.0 4.6 all-to-all-start.1
  51.8 12.1 %all-to-all-done.1 = bf16[8,16,1920]{2,1,0:T(8,128)(2,1)S(1)} async-done(((bf16[8,16,1920]{2,1,0:T(8,128)(2,1)}), bf16[8,16,1920]{2,1,0:T(8,128)(2,1)S(1)}, u32[]{:S(2)}, u32[]{:S(2)}) %all-to-all-start.1) | async-done | bytes 491552 | tf_op jit(solution)/shard_map/all_to_all | solution.py:437
  68.6 4.4 all-to-all-start.2
  74.6 7.8 %all-to-all-done.2 = bf16[16,32,384]{2,1,0:T(8,128)(2,1)S(1)} async-done(((bf16[16,32,384]{2,1,0:T(8,128)(2,1)}), bf16[16,32,384]{2,1,0:T(8,128)(2,1)S(1)}, u32[]{:S(2)}, u32[]{:S(2)}) %all-to-all-start.2) | async-done | bytes 393248 | tf_op jit(solution)/shard_map/all_to_all | solution.py:27
  90.0 6.2 %collective-permute-done = bf16[16,8,384]{2,1,0:T(8,128)(2,1)S(1)} collective-permute-done((bf16[16,8,384]{2,1,0:T(8,128)(2,1)S(1)}, bf16[16,8,384]{2,1,0:T(8,128)(2,1)S(1)}, u32[]{:S(2)}, u32[]{:S(2)}) %collective-permute-start) | collective-permute-done | bytes 98336 | tf_op jit(solution)/shard_map/ppermute | solution.py:23
  96.3 9.7 %shard_map.305 = (bf16[1024,384]{1,0:T(8,128)(2,1)S(1)}, f32[3,1024,128]{2,1,0:T(8,128)S(1)}, f32[1024,384]{1,0:T(8,128)S(1)}, f32[1024,384]{1,0:T(8,128)S(1)}, ...) custom-call(bf16[1024,384]{1,0:T(8,128)(2,1)S(1)} %pad_maximum_fusio, ...), custom_call_target="tpu_custom_call" | custom-call | bytes 180000000 | tf_op jit(solution)/shard_map/pallas_call | solution.py:530
  115.1 15.0 %all_to_all.52.pieces = f32[16,2,16,384]{3,2,1,0:T(8,128)} all-to-all(f32[16,2,16,384]{3,2,1,0:T(8,128)S(1)} %broadcast_in_dim.144), channel_id=1, replica_groups=mesh['row'=2,'z'=4,'y'=4,'x'=4] {'y','x'}, dimensions={0} | all-to-all | bytes 1572864 | tf_op jit(solution)/shard_map/all_to_all | solution.py:540
  146.2 3.6 collective-permute-start.2
  149.8 3.5 fusion.89.pre.pre_own
  163.0 6.1 %collective-permute-done.5 = bf16[64,2048]{1,0:T(8,128)(2,1)S(1)} collective-permute-done((bf16[64,2048]{1,0:T(8,128)(2,1)S(1)}, bf16[64,2048]{1,0:T(8,128)(2,1)S(1)}, u32[]{:S(2)}, u32[]{:S(2)}) %collective-permute-start.5) | collective-permute-done | bytes 262176 | tf_op jit(solution)/shard_map/ppermute | solution.py:23
  172.5 10.2 %collective-permute-done.6 = bf16[128,2048]{1,0:T(8,128)(2,1)} collective-permute-done((bf16[128,2048]{1,0:T(8,128)(2,1)S(1)}, bf16[128,2048]{1,0:T(8,128)(2,1)}, u32[]{:S(2)}, u32[]{:S(2)}) %collective-permute-start.6) | collective-permute-done | bytes 524320 | tf_op jit(solution)/shard_map/ppermute | solution.py:23
  182.8 3.4 collective-permute-done.4
  192.7 10.1 %collective-permute-done.7 = bf16[128,2048]{1,0:T(8,128)(2,1)S(1)} collective-permute-done((bf16[128,2048]{1,0:T(8,128)(2,1)S(1)}, bf16[128,2048]{1,0:T(8,128)(2,1)S(1)}, u32[]{:S(2)}, u32[]{:S(2)}) %collective-permute-start.7) | collective-permute-done | bytes 524320 | tf_op jit(solution)/shard_map/ppermute | solution.py:23
  212.2 13.7 %collective-permute-start.11 = (bf16[512,2048]{1,0:T(8,128)(2,1)}, bf16[512,2048]{1,0:T(8,128)(2,1)}, u32[]{:S(2)}, u32[]{:S(2)}) collective-permute-start(bf16[512,2048]{1,0:T(8,128)(2,1)} %bitcast.46), channel_id=1, source_target_pairs={{0,64},{64,0},{1,65},{65,1},{2,66},{66,2},{3,67},{67,3},{4,68},{68... | collective-permute-start | bytes 6291464 | tf_op jit(solution)/shard_map/ppermute | solution.py:23
  225.9 5.0 dynamic-slice_bitcast_fusion.1
  233.8 3.4 slice.471
  239.5 6.2 %fusion.139 = f32[512,1536]{1,0:T(8,128)S(1)} fusion(bf16[512,2048]{1,0:T(8,128)(2,1)} %collective-permute-done.11, bf16[2048,1536]{1,0:T(8,128)(2,1)S(1)} %bitcast.292), kind=kOutput, calls=%fused_computation.304 | convolution fusion | flops 3221225472 | bytes 11534336 | tf_op jit(solution)/shard_map/dot_general | solution.py:75
  248.4 4.7 convolution_convert_fusion.4
  253.8 5.0 fusion.138
  261.5 3.7 convolution_convert_fusion.5
  268.7 5.9 %collective-permute-done.15 = bf16[64,2048]{1,0:T(8,128)(2,1)S(1)} collective-permute-done((bf16[64,2048]{1,0:T(8,128)(2,1)S(1)}, bf16[64,2048]{1,0:T(8,128)(2,1)S(1)}, u32[]{:S(2)}, u32[]{:S(2)}) %collective-permute-start.15) | collective-permute-done | bytes 262176 | tf_op jit(solution)/shard_map/ppermute | solution.py:23
  278.9 10.8 %convolution_convert_fusion = bf16[2048,1536]{1,0:T(8,128)(2,1)S(1)} fusion(bf16[512,2048]{1,0:T(8,128)(2,1)} %collective-permute-done.11, bf16[512,2048]{1,0:T(8,128)(2,1)} %bitcast.46, bf16[512,768]{1,0:T(8,128)(2,1)} %copy-done.114, bf16[512,768]{1,0:T(8,128)(2,1)S(1)} %get-tuple-element.202, bf16[512,768]{1,0:T(8,128)(2,1)} %copy-done.116, ...), kind=kOutput, calls=%fused_computation.1 | convolution fusion | flops 6466568192 | bytes 13631488 | tf_op jit(solution)/shard_map/dot_general | solution.py:83
  298.7 3.7 fusion.25
  302.4 5.7 %collective-permute-done.17 = bf16[128,2048]{1,0:T(8,128)(2,1)S(1)} collective-permute-done((bf16[128,2048]{1,0:T(8,128)(2,1)S(1)}, bf16[128,2048]{1,0:T(8,128)(2,1)S(1)}, u32[]{:S(2)}, u32[]{:S(2)}) %collective-permute-start.17) | collective-permute-done | bytes 524320 | tf_op jit(solution)/shard_map/ppermute | solution.py:23
  312.2 9.5 %maximum_maximum_fusion = bf16[16,192,1536]{2,1,0:T(8,128)(2,1)} fusion(bf16[16,16,512]{2,1,0:T(8,128)(2,1)S(1)} %get-tuple-element.218, bf16[16,16,512]{2,1,0:T(8,128)(2,1)S(1)} %get-tuple-element.219, bf16[16,16,512]{2,1,0:T(8,128)(2,1)S(1)} %get-tuple-element.217, bf16[16,48,1536]{2,1,0:T(8,128)(2,1)S(1)} %slice.500, bf16[16,128,1536]{2,1,0:T(8,128)(2,1)S(1)} %bitcast.278), kind=kLoop, calls=%fused_computation | loop fusion | flops 47185920 | bytes 18874368 | tf_op jit(solution)/shard_map/concatenate | solution.py:625
  329.7 4.1 collective-permute-start.21
  333.8 4.0 collective-permute-done.21
  337.8 4.2 fusion.14
  345.9 4.9 all-to-all-start.4
  351.1 3.5 fusion.127.mixed_own
  357.2 7.6 %shard_map.309 = (bf16[1024,384]{1,0:T(8,128)(2,1)S(1)}, f32[3,1024,128]{2,1,0:T(8,128)S(1)}, f32[3,1024,128]{2,1,0:T(8,128)S(1)}, f32[2,16,384]{2,1,0:T(8,128)S(1)}) custom-call(f32[512,384]{1,0:T(8,128)S(1)} %fusion.127.mixed_own, f32[512,384]{1,0:T(8,128)S(1)} %fusion.125.mixed_other, f32[512,384]{1,0:T(8,128)S(1)} %copy-done.17, ...), custom_call_target="tpu_custom_call" | custom-call | bytes 300000000 | tf_op jit(solution)/shard_map/pallas_call | solution.py:643
  368.7 15.6 %all-to-all-done.4 = bf16[16,22,2048]{2,1,0:T(8,128)(2,1)} async-done(((bf16[16,22,2048]{2,1,0:T(8,128)(2,1)}), bf16[16,22,2048]{2,1,0:T(8,128)(2,1)}, u32[]{:S(2)}, u32[]{:S(2)}) %all-to-all-start.4) | async-done | bytes 1441824 | tf_op jit(solution)/shard_map/all_to_all | solution.py:654
  386.1 4.3 all-to-all-start.5
  390.5 3.4 fusion.6
  397.8 8.7 %all-to-all-done.5.pieces = f32[16,2,16,384]{3,2,1,0:T(8,128)} async-done(((f32[16,2,16,384]{3,2,1,0:T(8,128)}), f32[16,2,16,384]{3,2,1,0:T(8,128)}, u32[]{:S(2)}, u32[]{:S(2)}) %all-to-all-start.5) | async-done | bytes 786464 | tf_op jit(solution)/shard_map/all_to_all | solution.py:540
  408.3 4.4 all-to-all-start.6
  421.8 6.2 %shard_map.311 = (bf16[1024,384]{1,0:T(8,128)(2,1)S(1)}, bf16[1024,384]{1,0:T(8,128)(2,1)S(1)}, bf16[1024,384]{1,0:T(8,128)(2,1)S(1)}, f32[8,384]{1,0:T(8,128)S(1)}) custom-call(f32[3,1024,128]{2,1,0:T(8,128)S(1)} %copy-done.26, f32[3,1024,128]{2,1,0:T(8,128)S(1)} %copy-done.28, f32[16,1,384]{2,1,0:T(1,128)S(1)} %copy-done.40, f32[512,384]{1,0:T(8,128)S(1)} %copy-done.13, ...), custom_call_target="tpu_custom_call" | custom-call | bytes 300000000 | tf_op jit(solution)/shard_map/pallas_call | solution.py:659
  430.7 4.8 collective-permute-start.22
  435.5 4.9 convolution_convert_fusion.1
  455.3 4.3 convolution_convert_fusion.6
  461.4 6.1 %all-to-all-start.7 = ((bf16[16,160,384]{2,1,0:T(8,128)(2,1)}), bf16[16,160,384]{2,1,0:T(8,128)(2,1)S(1)}, u32[]{:S(2)}, u32[]{:S(2)}) async-start(bf16[16,160,384]{2,1,0:T(8,128)(2,1)} %pad_maximum_fusion.6), calls=%async_computation.9 | async-start | bytes 3932160 | tf_op jit(solution)/shard_map/all_to_all | solution.py:700
  467.5 3.5 convolution_convert_fusion.3
  477.9 11.7 %collective-permute-done.24 = bf16[64,2048]{1,0:T(8,128)(2,1)S(1)} collective-permute-done((bf16[64,2048]{1,0:T(8,128)(2,1)S(1)}, bf16[64,2048]{1,0:T(8,128)(2,1)S(1)}, u32[]{:S(2)}, u32[]{:S(2)}) %collective-permute-start.24) | collective-permute-done | bytes 262176 | tf_op jit(solution)/shard_map/ppermute | solution.py:23
  490.5 8.0 %all-to-all-done.7 = bf16[16,160,384]{2,1,0:T(8,128)(2,1)S(1)} async-done(((bf16[16,160,384]{2,1,0:T(8,128)(2,1)}), bf16[16,160,384]{2,1,0:T(8,128)(2,1)S(1)}, u32[]{:S(2)}, u32[]{:S(2)}) %all-to-all-start.7) | async-done | bytes 1966112 | tf_op jit(solution)/shard_map/all_to_all | solution.py:700
  523.2 7.6 %all-to-all-start.8 = ((bf16[8,16,2304]{2,1,0:T(8,128)(2,1)}), bf16[8,16,2304]{2,1,0:T(8,128)(2,1)S(1)}, u32[]{:S(2)}, u32[]{:S(2)}) async-start(bf16[8,16,2304]{2,1,0:T(8,128)(2,1)} %bitcast.96), calls=%async_computation.10 | async-start | bytes 1179648 | tf_op jit(solution)/shard_map/all_to_all | solution.py:612
  533.5 7.3 %all-to-all-done.8 = bf16[8,16,2304]{2,1,0:T(8,128)(2,1)S(1)} async-done(((bf16[8,16,2304]{2,1,0:T(8,128)(2,1)}), bf16[8,16,2304]{2,1,0:T(8,128)(2,1)S(1)}, u32[]{:S(2)}, u32[]{:S(2)}) %all-to-all-start.8) | async-done | bytes 589856 | tf_op jit(solution)/shard_map/all_to_all | solution.py:612
  (512 shorter events, 196.8 us)
Async XLA Ops:
  7.2 75.8 %all-gather.8.cloned.1.call-start = ((), (), s32[]{:S(2)}) async-start(), calls=%async_computation.11 | async-start | bytes 4718592 | tf_op jit(solution)/shard_map/all_gather | solution.py:413
  11.2 34.8 %all-to-all-start = ((bf16[128,16,384]{2,1,0:T(8,128)(2,1)}), bf16[128,16,384]{2,1,0:T(8,128)(2,1)S(1)}, u32[]{:S(2)}, u32[]{:S(2)}) async-start(bf16[128,16,384]{2,1,0:T(8,128)(2,1)} %bitcast.7), calls=%async_computation | async-start | bytes 3145728 | tf_op jit(solution)/shard_map/all_to_all | solution.py:427
  23.2 42.1 %copy-start.110 = (bf16[22]{0:T(256)(128)(2,1)S(1)}, bf16[22]{0:T(256)(128)(2,1)}, u32[]{:S(2)}) copy-start(bf16[22]{0:T(256)(128)(2,1)} %param.28) | copy-start | bytes 136
  23.3 42.2 %copy-start.111 = (bf16[22]{0:T(256)(128)(2,1)S(1)}, bf16[22]{0:T(256)(128)(2,1)}, u32[]{:S(2)}) copy-start(bf16[22]{0:T(256)(128)(2,1)} %param.29) | copy-start | bytes 136
  23.3 42.4 %copy-start.101 = (bf16[22,176]{1,0:T(8,128)(2,1)S(1)}, bf16[22,176]{1,0:T(8,128)(2,1)}, u32[]{:S(2)}) copy-start(bf16[22,176]{1,0:T(8,128)(2,1)} %param.25) | copy-start | bytes 23236
  23.3 42.4 %copy-start.102 = (bf16[22,176]{1,0:T(8,128)(2,1)S(1)}, bf16[22,176]{1,0:T(8,128)(2,1)}, u32[]{:S(2)}) copy-start(bf16[22,176]{1,0:T(8,128)(2,1)} %param.27) | copy-start | bytes 23236
  23.3 42.7 %copy-start.75 = (bf16[2,64,2048]{2,1,0:T(8,128)(2,1)S(1)}, bf16[2,64,2048]{2,1,0:T(8,128)(2,1)}, u32[]{:S(2)}) copy-start(bf16[2,64,2048]{2,1,0:T(8,128)(2,1)} %param.35) | copy-start | bytes 1572868
  47.0 16.9 %all-to-all-start.1 = ((bf16[8,16,1920]{2,1,0:T(8,128)(2,1)}), bf16[8,16,1920]{2,1,0:T(8,128)(2,1)S(1)}, u32[]{:S(2)}, u32[]{:S(2)}) async-start(bf16[8,16,1920]{2,1,0:T(8,128)(2,1)} %copy.151), calls=%async_computation.1 | async-start | bytes 983040 | tf_op jit(solution)/shard_map/all_to_all | solution.py:437
  51.6 80.5 %all-gather.10.cloned.1.call-start = ((), (), s32[]{:S(2)}) async-start(), calls=%async_computation.14 | async-start | bytes 4177920 | tf_op jit(solution)/shard_map/all_gather | solution.py:453
  64.6 2.3 collective-permute-start.1
  68.6 13.8 %all-to-all-start.2 = ((bf16[16,32,384]{2,1,0:T(8,128)(2,1)}), bf16[16,32,384]{2,1,0:T(8,128)(2,1)S(1)}, u32[]{:S(2)}, u32[]{:S(2)}) async-start(bf16[16,32,384]{2,1,0:T(8,128)(2,1)} %broadcast_in_dim.141), calls=%async_computation.2 | async-start | bytes 786432 | tf_op jit(solution)/shard_map/all_to_all | solution.py:27
  73.0 152.9 %all-gather.14.cloned.1.call-start = ((), (), s32[]{:S(2)}) async-start(), calls=%async_computation.16 | async-start | bytes 4718592 | tf_op jit(solution)/shard_map/all_gather | solution.py:413
  89.3 6.9 %collective-permute-start = (bf16[16,8,384]{2,1,0:T(8,128)(2,1)S(1)}, bf16[16,8,384]{2,1,0:T(8,128)(2,1)S(1)}, u32[]{:S(2)}, u32[]{:S(2)}) collective-permute-start(bf16[16,8,384]{2,1,0:T(8,128)(2,1)S(1)} %slice.452), channel_id=1, source_target_pairs={{0,1},{1,2},{2,3},{3,4},{4,5},{5,6},{6,7},{7,8},{8,9},{9,10},{10,1... | collective-permute-start | bytes 294920 | tf_op jit(solution)/shard_map/ppermute | solution.py:23
  114.0 118.0 %all-gather.12.cloned.1.call-start = ((), (), s32[]{:S(2)}) async-start(), calls=%async_computation.15 | async-start | bytes 10027008 | tf_op jit(solution)/shard_map/all_gather | solution.py:460
  115.0 406.2 %reduce-scatter.5.cloned.1.call-start = ((), (), s32[]{:S(2)}) async-start(), calls=%async_computation.13 | async-start | bytes 10027008 | tf_op jit(solution)/shard_map/reduce_scatter | solution.py:638
  146.2 9.0 %collective-permute-start.2 = (bf16[512,2048]{1,0:T(8,128)(2,1)}, bf16[512,2048]{1,0:T(8,128)(2,1)}, u32[]{:S(2)}, u32[]{:S(2)}) collective-permute-start(bf16[512,2048]{1,0:T(8,128)(2,1)} %get-tuple-element.60), channel_id=1, source_target_pairs={{0,64},{64,0},{1,65},{65,1},{2,66},{66,2},{3,67},{67,3},{4,68},{68... | collective-permute-start | bytes 6291464 | tf_op jit(solution)/shard_map/ppermute | solution.py:23
  158.4 13.9 %collective-permute-start.3 = (bf16[64,2048]{1,0:T(8,128)(2,1)S(1)}, bf16[64,2048]{1,0:T(8,128)(2,1)S(1)}, u32[]{:S(2)}, u32[]{:S(2)}) collective-permute-start(bf16[64,2048]{1,0:T(8,128)(2,1)S(1)} %get-tuple-element.231), channel_id=1, source_target_pairs={{0,16},{16,32},{32,48},{48,0},{1,17},{17,33},{33,49},{49,1},{2,18}... | collective-permute-start | bytes 786440 | tf_op jit(solution)/shard_map/ppermute | solution.py:23
  161.6 7.6 %collective-permute-start.5 = (bf16[64,2048]{1,0:T(8,128)(2,1)S(1)}, bf16[64,2048]{1,0:T(8,128)(2,1)S(1)}, u32[]{:S(2)}, u32[]{:S(2)}) collective-permute-start(bf16[64,2048]{1,0:T(8,128)(2,1)S(1)} %get-tuple-element.232), channel_id=1, source_target_pairs={{0,48},{16,0},{32,16},{48,32},{1,49},{17,1},{33,17},{49,33},{2,50}... | collective-permute-start | bytes 786440 | tf_op jit(solution)/shard_map/ppermute | solution.py:23
  169.3 13.5 %collective-permute-start.6 = (bf16[128,2048]{1,0:T(8,128)(2,1)S(1)}, bf16[128,2048]{1,0:T(8,128)(2,1)}, u32[]{:S(2)}, u32[]{:S(2)}) collective-permute-start(bf16[128,2048]{1,0:T(8,128)(2,1)S(1)} %pad_maximum_fusion.11), channel_id=1, source_target_pairs={{0,48},{16,0},{32,16},{48,32},{1,49},{17,1},{33,17},{49,33},{2,50}... | collective-permute-start | bytes 1572872 | tf_op jit(solution)/shard_map/ppermute | solution.py:23
  172.4 13.7 %collective-permute-start.4 = (bf16[128,2048]{1,0:T(8,128)(2,1)S(1)}, bf16[128,2048]{1,0:T(8,128)(2,1)}, u32[]{:S(2)}, u32[]{:S(2)}) collective-permute-start(bf16[128,2048]{1,0:T(8,128)(2,1)S(1)} %pad_maximum_fusion.10), channel_id=1, source_target_pairs={{0,16},{16,32},{32,48},{48,0},{1,17},{17,33},{33,49},{49,1},{2,18}... | collective-permute-start | bytes 1572872 | tf_op jit(solution)/shard_map/ppermute | solution.py:23
  188.2 105.0 %copy-start.50 = (f32[128,2048]{1,0:T(8,128)}, f32[128,2048]{1,0:T(8,128)S(1)}, u32[]{:S(2)}) copy-start(f32[128,2048]{1,0:T(8,128)S(1)} %get-tuple-element.196) | copy-start | bytes 3145732
  191.2 11.5 %collective-permute-start.7 = (bf16[128,2048]{1,0:T(8,128)(2,1)S(1)}, bf16[128,2048]{1,0:T(8,128)(2,1)S(1)}, u32[]{:S(2)}, u32[]{:S(2)}) collective-permute-start(bf16[128,2048]{1,0:T(8,128)(2,1)S(1)} %get-tuple-element.194), channel_id=1, source_target_pairs={{0,48},{16,0},{32,16},{48,32},{1,49},{17,1},{33,17},{49,33},{2,50}... | collective-permute-start | bytes 1572872 | tf_op jit(solution)/shard_map/ppermute | solution.py:23
  191.3 13.2 %collective-permute-start.8 = (bf16[128,2048]{1,0:T(8,128)(2,1)S(1)}, bf16[128,2048]{1,0:T(8,128)(2,1)S(1)}, u32[]{:S(2)}, u32[]{:S(2)}) collective-permute-start(bf16[128,2048]{1,0:T(8,128)(2,1)S(1)} %get-tuple-element.194), channel_id=1, source_target_pairs={{0,16},{16,32},{32,48},{48,0},{1,17},{17,33},{33,49},{49,1},{2,18}... | collective-permute-start | bytes 1572872 | tf_op jit(solution)/shard_map/ppermute | solution.py:23
  202.8 5.7 %collective-permute-start.10 = (bf16[64,2048]{1,0:T(8,128)(2,1)S(1)}, bf16[64,2048]{1,0:T(8,128)(2,1)S(1)}, u32[]{:S(2)}, u32[]{:S(2)}) collective-permute-start(bf16[64,2048]{1,0:T(8,128)(2,1)S(1)} %slice.469), channel_id=1, source_target_pairs={{0,48},{16,0},{32,16},{48,32},{1,49},{17,1},{33,17},{49,33},{2,50}... | collective-permute-start | bytes 786440 | tf_op jit(solution)/shard_map/ppermute | solution.py:23
  204.5 6.9 %collective-permute-start.9 = (bf16[64,2048]{1,0:T(8,128)(2,1)S(1)}, bf16[64,2048]{1,0:T(8,128)(2,1)S(1)}, u32[]{:S(2)}, u32[]{:S(2)}) collective-permute-start(bf16[64,2048]{1,0:T(8,128)(2,1)S(1)} %slice.468), channel_id=1, source_target_pairs={{0,16},{16,32},{32,48},{48,0},{1,17},{17,33},{33,49},{49,1},{2,18}... | collective-permute-start | bytes 786440 | tf_op jit(solution)/shard_map/ppermute | solution.py:23
  212.2 27.3 %collective-permute-start.11 = (bf16[512,2048]{1,0:T(8,128)(2,1)}, bf16[512,2048]{1,0:T(8,128)(2,1)}, u32[]{:S(2)}, u32[]{:S(2)}) collective-permute-start(bf16[512,2048]{1,0:T(8,128)(2,1)} %bitcast.46), channel_id=1, source_target_pairs={{0,64},{64,0},{1,65},{65,1},{2,66},{66,2},{3,67},{67,3},{4,68},{68... | collective-permute-start | bytes 6291464 | tf_op jit(solution)/shard_map/ppermute | solution.py:23
  253.1 12.1 %collective-permute-start.12 = (bf16[512,2048]{1,0:T(8,128)(2,1)}, bf16[512,2048]{1,0:T(8,128)(2,1)S(1)}, u32[]{:S(2)}, u32[]{:S(2)}) collective-permute-start(bf16[512,2048]{1,0:T(8,128)(2,1)} %convolution_convert_fusion.4), channel_id=1, source_target_pairs={{0,64},{64,0},{1,65},{65,1},{2,66},{66,2},{3,67},{67,3},{4,68},{68... | collective-permute-start | bytes 6291464 | tf_op jit(solution)/shard_map/ppermute | solution.py:23
  265.9 12.4 %collective-permute-start.13 = (bf16[64,2048]{1,0:T(8,128)(2,1)S(1)}, bf16[64,2048]{1,0:T(8,128)(2,1)S(1)}, u32[]{:S(2)}, u32[]{:S(2)}) collective-permute-start(bf16[64,2048]{1,0:T(8,128)(2,1)S(1)} %get-tuple-element.229), channel_id=1, source_target_pairs={{0,16},{16,32},{32,48},{48,0},{1,17},{17,33},{33,49},{49,1},{2,18}... | collective-permute-start | bytes 786440 | tf_op jit(solution)/shard_map/ppermute | solution.py:23
  267.2 7.4 %collective-permute-start.15 = (bf16[64,2048]{1,0:T(8,128)(2,1)S(1)}, bf16[64,2048]{1,0:T(8,128)(2,1)S(1)}, u32[]{:S(2)}, u32[]{:S(2)}) collective-permute-start(bf16[64,2048]{1,0:T(8,128)(2,1)S(1)} %get-tuple-element.230), channel_id=1, source_target_pairs={{0,48},{16,0},{32,16},{48,32},{1,49},{17,1},{33,17},{49,33},{2,50}... | collective-permute-start | bytes 786440 | tf_op jit(solution)/shard_map/ppermute | solution.py:23
  275.5 16.2 %collective-permute-start.16 = (bf16[128,2048]{1,0:T(8,128)(2,1)}, bf16[128,2048]{1,0:T(8,128)(2,1)S(1)}, u32[]{:S(2)}, u32[]{:S(2)}) collective-permute-start(bf16[128,2048]{1,0:T(8,128)(2,1)} %pad_maximum_fusion.13), channel_id=1, source_target_pairs={{0,48},{16,0},{32,16},{48,32},{1,49},{17,1},{33,17},{49,33},{2,50}... | collective-permute-start | bytes 1572872 | tf_op jit(solution)/shard_map/ppermute | solution.py:23
  278.4 13.6 %collective-permute-start.14 = (bf16[128,2048]{1,0:T(8,128)(2,1)S(1)}, bf16[128,2048]{1,0:T(8,128)(2,1)S(1)}, u32[]{:S(2)}, u32[]{:S(2)}) collective-permute-start(bf16[128,2048]{1,0:T(8,128)(2,1)S(1)} %pad_maximum_fusion.12), channel_id=1, source_target_pairs={{0,16},{16,32},{32,48},{48,0},{1,17},{17,33},{33,49},{49,1},{2,18}... | collective-permute-start | bytes 1572872 | tf_op jit(solution)/shard_map/ppermute | solution.py:23
  296.1 12.0 %collective-permute-start.17 = (bf16[128,2048]{1,0:T(8,128)(2,1)S(1)}, bf16[128,2048]{1,0:T(8,128)(2,1)S(1)}, u32[]{:S(2)}, u32[]{:S(2)}) collective-permute-start(bf16[128,2048]{1,0:T(8,128)(2,1)S(1)} %get-tuple-element.189), channel_id=1, source_target_pairs={{0,48},{16,0},{32,16},{48,32},{1,49},{17,1},{33,17},{49,33},{2,50}... | collective-permute-start | bytes 1572872 | tf_op jit(solution)/shard_map/ppermute | solution.py:23
  298.7 12.6 %collective-permute-start.18 = (bf16[128,2048]{1,0:T(8,128)(2,1)S(1)}, bf16[128,2048]{1,0:T(8,128)(2,1)S(1)}, u32[]{:S(2)}, u32[]{:S(2)}) collective-permute-start(bf16[128,2048]{1,0:T(8,128)(2,1)S(1)} %get-tuple-element.189), channel_id=1, source_target_pairs={{0,16},{16,32},{32,48},{48,0},{1,17},{17,33},{33,49},{49,1},{2,18}... | collective-permute-start | bytes 1572872 | tf_op jit(solution)/shard_map/ppermute | solution.py:23
  321.8 5.5 collective-permute-start.20
  322.4 6.5 %collective-permute-start.19 = (bf16[64,2048]{1,0:T(8,128)(2,1)S(1)}, bf16[64,2048]{1,0:T(8,128)(2,1)S(1)}, u32[]{:S(2)}, u32[]{:S(2)}) collective-permute-start(bf16[64,2048]{1,0:T(8,128)(2,1)S(1)} %slice.486), channel_id=1, source_target_pairs={{0,16},{16,32},{32,48},{48,0},{1,17},{17,33},{33,49},{49,1},{2,18}... | collective-permute-start | bytes 786440 | tf_op jit(solution)/shard_map/ppermute | solution.py:23
  329.7 8.1 %collective-permute-start.21 = (bf16[512,2048]{1,0:T(8,128)(2,1)}, bf16[512,2048]{1,0:T(8,128)(2,1)S(1)}, u32[]{:S(2)}, u32[]{:S(2)}) collective-permute-start(bf16[512,2048]{1,0:T(8,128)(2,1)} %bitcast.322), channel_id=1, source_target_pairs={{0,64},{64,0},{1,65},{65,1},{2,66},{66,2},{3,67},{67,3},{4,68},{68... | collective-permute-start | bytes 6291464 | tf_op jit(solution)/shard_map/ppermute | solution.py:23
  345.9 38.5 %all-to-all-start.4 = ((bf16[16,22,2048]{2,1,0:T(8,128)(2,1)}), bf16[16,22,2048]{2,1,0:T(8,128)(2,1)}, u32[]{:S(2)}, u32[]{:S(2)}) async-start(bf16[16,22,2048]{2,1,0:T(8,128)(2,1)} %reshape.752), calls=%async_computation.4 | async-start | bytes 3145728 | tf_op jit(solution)/shard_map/all_to_all | solution.py:654
  386.1 20.3 %all-to-all-start.5 = ((f32[16,2,16,384]{3,2,1,0:T(8,128)}), f32[16,2,16,384]{3,2,1,0:T(8,128)}, u32[]{:S(2)}, u32[]{:S(2)}) async-start(f32[16,2,16,384]{3,2,1,0:T(8,128)} %broadcast_in_dim.153), calls=%async_computation.5 | async-start | bytes 1572864 | tf_op jit(solution)/shard_map/all_to_all | solution.py:540
  408.3 35.3 %all-to-all-start.6 = ((bf16[16,128,384]{2,1,0:T(8,128)(2,1)}), bf16[16,128,384]{2,1,0:T(8,128)(2,1)}, u32[]{:S(2)}, u32[]{:S(2)}) async-start(bf16[16,128,384]{2,1,0:T(8,128)(2,1)} %bitcast.296), calls=%async_computation.7 | async-start | bytes 3145728 | tf_op jit(solution)/shard_map/all_to_all | solution.py:658
  412.7 118.0 %reduce-scatter.3.cloned.1.call-start = ((), (), s32[]{:S(2)}) async-start(), calls=%async_computation.12 | async-start | bytes 4718592 | tf_op jit(solution)/shard_map/reduce_scatter | solution.py:668
  430.7 9.9 %collective-permute-start.22 = (bf16[16,8,384]{2,1,0:T(8,128)(2,1)S(1)}, bf16[16,8,384]{2,1,0:T(8,128)(2,1)S(1)}, u32[]{:S(2)}, u32[]{:S(2)}) collective-permute-start(bf16[16,8,384]{2,1,0:T(8,128)(2,1)S(1)} %slice.489), channel_id=1, source_target_pairs={{0,15},{1,0},{2,1},{3,2},{4,3},{5,4},{6,5},{7,6},{8,7},{9,8},{10,9... | collective-permute-start | bytes 294920 | tf_op jit(solution)/shard_map/ppermute | solution.py:23
  448.7 22.3 %collective-permute-start.23 = (bf16[512,2048]{1,0:T(8,128)(2,1)}, bf16[512,2048]{1,0:T(8,128)(2,1)}, u32[]{:S(2)}, u32[]{:S(2)}) collective-permute-start(bf16[512,2048]{1,0:T(8,128)(2,1)} %convolution_convert_fusion.2), channel_id=1, source_target_pairs={{0,64},{64,0},{1,65},{65,1},{2,66},{66,2},{3,67},{67,3},{4,68},{68... | collective-permute-start | bytes 6291464 | tf_op jit(solution)/shard_map/ppermute | solution.py:23
  461.4 37.2 %all-to-all-start.7 = ((bf16[16,160,384]{2,1,0:T(8,128)(2,1)}), bf16[16,160,384]{2,1,0:T(8,128)(2,1)S(1)}, u32[]{:S(2)}, u32[]{:S(2)}) async-start(bf16[16,160,384]{2,1,0:T(8,128)(2,1)} %pad_maximum_fusion.6), calls=%async_computation.9 | async-start | bytes 3932160 | tf_op jit(solution)/shard_map/all_to_all | solution.py:700
  474.5 15.2 %collective-permute-start.24 = (bf16[64,2048]{1,0:T(8,128)(2,1)S(1)}, bf16[64,2048]{1,0:T(8,128)(2,1)S(1)}, u32[]{:S(2)}, u32[]{:S(2)}) collective-permute-start(bf16[64,2048]{1,0:T(8,128)(2,1)S(1)} %get-tuple-element.227), channel_id=1, source_target_pairs={{0,16},{16,32},{32,48},{48,0},{1,17},{17,33},{33,49},{49,1},{2,18}... | collective-permute-start | bytes 786440 | tf_op jit(solution)/shard_map/ppermute | solution.py:23
  474.5 26.4 %collective-permute-start.26 = (bf16[64,2048]{1,0:T(8,128)(2,1)}, bf16[64,2048]{1,0:T(8,128)(2,1)}, u32[]{:S(2)}, u32[]{:S(2)}) collective-permute-start(bf16[64,2048]{1,0:T(8,128)(2,1)} %get-tuple-element.228), channel_id=1, source_target_pairs={{0,48},{16,0},{32,16},{48,32},{1,49},{17,1},{33,17},{49,33},{2,50}... | collective-permute-start | bytes 786440 | tf_op jit(solution)/shard_map/ppermute | solution.py:23
  500.2 16.5 %collective-permute-start.25 = (bf16[128,2048]{1,0:T(8,128)(2,1)}, bf16[128,2048]{1,0:T(8,128)(2,1)S(1)}, u32[]{:S(2)}, u32[]{:S(2)}) collective-permute-start(bf16[128,2048]{1,0:T(8,128)(2,1)} %pad_maximum_fusion.14), channel_id=1, source_target_pairs={{0,16},{16,32},{32,48},{48,0},{1,17},{17,33},{33,49},{49,1},{2,18}... | collective-permute-start | bytes 1572872 | tf_op jit(solution)/shard_map/ppermute | solution.py:23
  503.8 12.9 %collective-permute-start.27 = (bf16[128,2048]{1,0:T(8,128)(2,1)}, bf16[128,2048]{1,0:T(8,128)(2,1)}, u32[]{:S(2)}, u32[]{:S(2)}) collective-permute-start(bf16[128,2048]{1,0:T(8,128)(2,1)} %pad_maximum_fusion.15), channel_id=1, source_target_pairs={{0,48},{16,0},{32,16},{48,32},{1,49},{17,1},{33,17},{49,33},{2,50}... | collective-permute-start | bytes 1572872 | tf_op jit(solution)/shard_map/ppermute | solution.py:23
  523.2 17.6 %all-to-all-start.8 = ((bf16[8,16,2304]{2,1,0:T(8,128)(2,1)}), bf16[8,16,2304]{2,1,0:T(8,128)(2,1)S(1)}, u32[]{:S(2)}, u32[]{:S(2)}) async-start(bf16[8,16,2304]{2,1,0:T(8,128)(2,1)} %bitcast.96), calls=%async_computation.10 | async-start | bytes 1179648 | tf_op jit(solution)/shard_map/all_to_all | solution.py:612
  (113 other events, 722.3 us)
Sparse Core Ops, SparseCore 0:
  9.7 57.8 all-gather.7
  70.3 49.2 all-gather.9
  121.9 32.4 all-gather.13
  157.0 74.9 all-gather.11
  321.9 123.6 reduce-scatter.4
  447.9 57.2 reduce-scatter.2
